TPU v7x, 32 devices: a whole 2x2x4 slice. The times are simulated.
32 devices in a mesh: grp: 2 (over y), rep: 16 (over z, x, core).
Axes of the slice: x: 2, y: 2, z: 4, core: 2. Of those that a mesh axis runs over, the one named last changes fastest.
Arguments:
- tokens: bfloat16 [4096, 1280], P(('grp', 'rep')), may hold values from -6 to 6
- doc_ids: int32 [2, 2048], P('grp'), may hold values from 0 to 3, never falling along the last dimension, each value on 1 to 1152 neighbouring positions
- w_query: bfloat16 [1280, 1280], P('grp'), may hold values from -0.15625 to 0.15625
- w_key: bfloat16 [1280, 1280], P('grp'), may hold values from -0.15625 to 0.15625
- w_value: bfloat16 [1280, 1280], P('grp'), may hold values from -0.15625 to 0.15625
- w_out: bfloat16 [1280, 1280], P('grp'), may hold values from -1 to 1
- w_up: bfloat16 [1280, 5120], P('grp'), may hold values from -0.15625 to 0.15625
- w_down: bfloat16 [5120, 1280], P('grp'), may hold values from -0.078125 to 0.078125
- b_query: bfloat16 [1280], P('grp'), may hold values from -3 to 3
- b_value: bfloat16 [1280], P('grp'), may hold values from -3 to 3
- b_out: bfloat16 [1280], P('grp'), may hold values from -2 to 2
- b_up: bfloat16 [5120], P('grp'), may hold values from -3 to 3
- b_down: bfloat16 [1280], P('grp'), may hold values from -2 to 2
- attn_gain: bfloat16 [1280], P('grp'), may hold values from 0.5 to 1.5
- attn_beta: bfloat16 [1280], P('grp'), may hold values from -2 to 2
- ffn_gain: bfloat16 [1280], P('grp'), may hold values from 0.5 to 1.5
- ffn_beta: bfloat16 [1280], P('grp'), may hold values from -2 to 2
- cotangent: bfloat16 [4096, 1280], P(('grp', 'rep')), may hold values from -6 to 6
Outputs:
- output: bfloat16 [4096, 1280], P(('grp', 'rep'))
- grad_input: float32 [4096, 1280], P(('grp', 'rep'))
- grad_w_query: float32 [1280, 1280], P('grp')
- grad_w_key: float32 [1280, 1280], P('grp')
- grad_w_value: float32 [1280, 1280], P('grp')
- grad_w_out: float32 [1280, 1280], P('grp')
- grad_w_up: float32 [1280, 5120], P('grp')
- grad_w_down: float32 [5120, 1280], P('grp')
- grad_b_query: float32 [1280], P('grp')
- grad_b_value: float32 [1280], P('grp')
- grad_b_out: float32 [1280], P('grp')
- grad_b_up: float32 [5120], P('grp')
- grad_b_down: float32 [1280], P('grp')
- grad_attn_gain: float32 [1280], P('grp')
- grad_attn_beta: float32 [1280], P('grp')
- grad_ffn_gain: float32 [1280], P('grp')
- grad_ffn_beta: float32 [1280], P('grp')
Inputs may be any that keep to these rules, and one draw needn't show every extreme that they name: `doc_ids`: in each row, document numbers start at 0 and never fall; every document 0 to 3 has 1 to 1152 tokens, and some document has exactly 1152.
All inputs are finite; a program needn't handle non-finite values.
Results may differ from a plain program's by a relative error of at most 0.02.
Values may be sent and summed in bfloat16 or wider, within the bound.
A program may use at most 256 MiB of HBM per device.

v0:
```python
import jax
import jax.numpy as jnp
from jax import lax
from jax.sharding import PartitionSpec as P

HEADS = 20
HEAD_DIM = 64
PAIRS = 4


EPSILON = 1e-05
NEGATIVE = -1e30
GELU_SCALE = 0.7978845608028654
GELU_CUBIC = 0.044715


def from_behind(array, axis, by):
    length = lax.axis_size(axis)
    pairs = [(i, i + by) for i in range(length) if 0 <= i + by < length]
    return lax.ppermute(array, axis, pairs)


def passed_along(block, axis, distance):
    devices = range(lax.axis_size(axis))
    route = [((i - distance) % len(devices), i) for i in devices]
    return lax.ppermute(block, axis, route)


def norm_rows(values):
    center = values - jnp.mean(values, axis=-1, keepdims=True)
    inverse = lax.rsqrt(jnp.mean(center * center, axis=-1, keepdims=True) + EPSILON)
    return (center * inverse, inverse)


def norm_grad(grad_norm, normed, inverse, gain):
    scaled = grad_norm * gain
    return inverse * (
        scaled
        - jnp.mean(scaled, axis=-1, keepdims=True)
        - normed * jnp.mean(scaled * normed, axis=-1, keepdims=True)
    )


def gelu_pair(inputs):
    inner = jnp.tanh(GELU_SCALE * (inputs + GELU_CUBIC * inputs * inputs * inputs))
    value = 0.5 * inputs * (1.0 + inner)
    slope = 0.5 * (1.0 + inner) + 0.5 * inputs * (1.0 - inner * inner) * GELU_SCALE * (
        1.0 + 3.0 * GELU_CUBIC * inputs * inputs
    )
    return (value, slope)


def matmul(left, right):
    return jnp.dot(left, right, preferred_element_type=jnp.float32)


def matmul_tn(left, right):
    return lax.dot_general(
        left, right, (((0,), (0,)), ((), ())), preferred_element_type=jnp.float32
    )


def matmul_nt(left, right):
    return lax.dot_general(
        left, right, (((1,), (1,)), ((), ())), preferred_element_type=jnp.float32
    )


def shards(
    tokens,
    doc_ids,
    w_query,
    w_key,
    w_value,
    w_out,
    w_up,
    w_down,
    b_query,
    b_value,
    b_out,
    b_up,
    b_down,
    attn_gain,
    attn_beta,
    ffn_gain,
    ffn_beta,
    cotangent,
):
    tok_dev = tokens.shape[0]
    width = tokens.shape[1]
    scale = HEAD_DIM ** (-0.5)
    (
        full_query,
        full_key,
        full_value,
        full_out,
        full_up,
        full_down,
        bias_query,
        bias_value,
        bias_out,
        bias_up,
        bias_down,
        gain_attn,
        beta_attn,
        gain_ffn,
        beta_ffn,
    ) = (
        lax.all_gather(w_query, "grp", axis=0, tiled=True),
        lax.all_gather(w_key, "grp", axis=0, tiled=True),
        lax.all_gather(w_value, "grp", axis=0, tiled=True),
        lax.all_gather(w_out, "grp", axis=0, tiled=True),
        lax.all_gather(w_up, "grp", axis=0, tiled=True),
        lax.all_gather(w_down, "grp", axis=0, tiled=True),
        lax.all_gather(b_query, "grp", axis=0, tiled=True),
        lax.all_gather(b_value, "grp", axis=0, tiled=True),
        lax.all_gather(b_out, "grp", axis=0, tiled=True),
        lax.all_gather(b_up, "grp", axis=0, tiled=True),
        lax.all_gather(b_down, "grp", axis=0, tiled=True),
        lax.all_gather(attn_gain, "grp", axis=0, tiled=True),
        lax.all_gather(attn_beta, "grp", axis=0, tiled=True),
        lax.all_gather(ffn_gain, "grp", axis=0, tiled=True),
        lax.all_gather(ffn_beta, "grp", axis=0, tiled=True),
    )
    rep_index = lax.axis_index("rep")
    pad_front = (2 * PAIRS + 1) * tok_dev
    row_ids = doc_ids[0]
    padded_ids = jnp.concatenate([jnp.full((pad_front,), -1, jnp.int32), row_ids])
    query_pos = rep_index * tok_dev + jnp.arange(tok_dev, dtype=jnp.int32)
    query_doc = lax.dynamic_slice_in_dim(row_ids, rep_index * tok_dev, tok_dev)

    def block_mask(block_index):
        first = (rep_index - 2 * block_index - 1) * tok_dev
        key_pos = first + jnp.arange(2 * tok_dev, dtype=jnp.int32)
        key_doc = lax.dynamic_slice_in_dim(padded_ids, first + pad_front, 2 * tok_dev)
        return (key_doc[None, :] == query_doc[:, None]) & (key_pos[None, :] <= query_pos[:, None])

    xfull = tokens.astype(jnp.float32)
    normed_one, inverse_one = norm_rows(xfull)
    ln_one = (normed_one * gain_attn.astype(jnp.float32) + beta_attn.astype(jnp.float32)).astype(
        jnp.bfloat16
    )
    query = (matmul(ln_one, full_query) + bias_query.astype(jnp.float32)).astype(jnp.bfloat16)
    keys = matmul(ln_one, full_key).astype(jnp.bfloat16)
    values = (matmul(ln_one, full_value) + bias_value.astype(jnp.float32)).astype(jnp.bfloat16)
    query_heads = query.reshape(tok_dev, HEADS, HEAD_DIM)
    earlier = from_behind((keys, values), "rep", 1)
    first_block = (
        jnp.concatenate([earlier[0], keys], axis=0),
        jnp.concatenate([earlier[1], values], axis=0),
    )

    def fetch_pair(block, unused):
        moved = from_behind((block[0], block[1]), "rep", 2)
        return (moved, moved)

    unused_end, following = lax.scan(fetch_pair, first_block, None, length=PAIRS)
    key_blocks = jnp.concatenate([first_block[0][None], following[0]], axis=0)
    value_blocks = jnp.concatenate([first_block[1][None], following[1]], axis=0)
    block_numbers = jnp.arange(PAIRS + 1, dtype=jnp.int32)

    def scores_of(block_keys, block_index):
        raw = (
            jnp.einsum(
                "qhd,khd->hqk",
                query_heads,
                block_keys.reshape(-1, HEADS, HEAD_DIM),
                preferred_element_type=jnp.float32,
            )
            * scale
        )
        return jnp.where(block_mask(block_index)[None], raw, NEGATIVE)

    def max_step(state, inputs):
        run_max, run_sum = state
        block_keys, block_index = inputs
        scores = scores_of(block_keys, block_index)
        new_max = jnp.maximum(run_max, jnp.max(scores, axis=-1))
        run_sum = run_sum * jnp.exp(run_max - new_max) + jnp.sum(
            jnp.exp(scores - new_max[..., None]), axis=-1
        )
        return ((new_max, run_sum), None)

    start_state = (
        jnp.full((HEADS, tok_dev), NEGATIVE, jnp.float32),
        jnp.zeros((HEADS, tok_dev), jnp.float32),
    )
    (top_score, total_exp), unused_max = lax.scan(
        max_step, start_state, (key_blocks, block_numbers)
    )
    log_total = top_score + jnp.log(total_exp)

    def value_step(total, inputs):
        block_keys, block_values, block_index = inputs
        probs = jnp.exp(scores_of(block_keys, block_index) - log_total[..., None]).astype(
            jnp.bfloat16
        )
        return (
            total
            + jnp.einsum(
                "hqk,khd->qhd",
                probs,
                block_values.reshape(-1, HEADS, HEAD_DIM),
                preferred_element_type=jnp.float32,
            ),
            None,
        )

    attn, unused_value = lax.scan(
        value_step,
        jnp.zeros((tok_dev, HEADS, HEAD_DIM), jnp.float32),
        (key_blocks, value_blocks, block_numbers),
    )
    attn_low = attn.reshape(tok_dev, width).astype(jnp.bfloat16)
    hidden = xfull + matmul(attn_low, full_out) + bias_out.astype(jnp.float32)
    normed_two, inverse_two = norm_rows(hidden)
    ln_two = (normed_two * gain_ffn.astype(jnp.float32) + beta_ffn.astype(jnp.float32)).astype(
        jnp.bfloat16
    )
    pre_act = matmul(ln_two, full_up) + bias_up.astype(jnp.float32)
    act_value, act_slope = gelu_pair(pre_act)
    act_low = act_value.astype(jnp.bfloat16)
    result = hidden + matmul(act_low, full_down) + bias_down.astype(jnp.float32)
    output = result.astype(jnp.bfloat16)
    (
        back_query,
        back_key,
        back_value,
        back_out,
        back_up,
        back_down,
        back_gain_attn,
        back_gain_ffn,
    ) = (
        lax.all_gather(w_query, "grp", axis=0, tiled=True),
        lax.all_gather(w_key, "grp", axis=0, tiled=True),
        lax.all_gather(w_value, "grp", axis=0, tiled=True),
        lax.all_gather(w_out, "grp", axis=0, tiled=True),
        lax.all_gather(w_up, "grp", axis=0, tiled=True),
        lax.all_gather(w_down, "grp", axis=0, tiled=True),
        lax.all_gather(attn_gain, "grp", axis=0, tiled=True),
        lax.all_gather(ffn_gain, "grp", axis=0, tiled=True),
    )
    grad_res = cotangent.astype(jnp.float32)
    grad_w_down = matmul_tn(act_low, cotangent)
    grad_b_down = jnp.sum(grad_res, axis=0)
    grad_pre = (matmul_nt(cotangent, back_down) * act_slope).astype(jnp.bfloat16)
    grad_w_up = matmul_tn(ln_two, grad_pre)
    grad_b_up = jnp.sum(grad_pre.astype(jnp.float32), axis=0)
    grad_ln_two = matmul_nt(grad_pre, back_up)
    grad_ffn_gain = jnp.sum(grad_ln_two * normed_two, axis=0)
    grad_ffn_beta = jnp.sum(grad_ln_two, axis=0)
    grad_hidden = grad_res + norm_grad(
        grad_ln_two, normed_two, inverse_two, back_gain_ffn.astype(jnp.float32)
    )
    grad_mix = grad_hidden.astype(jnp.bfloat16)
    grad_w_out = matmul_tn(attn_low, grad_mix)
    grad_b_out = jnp.sum(grad_mix.astype(jnp.float32), axis=0)
    grad_heads = (
        matmul_nt(grad_mix, back_out).astype(jnp.bfloat16).reshape(tok_dev, HEADS, HEAD_DIM)
    )
    delta = jnp.sum(grad_heads.astype(jnp.float32) * attn, axis=-1).T

    def block_grads(block_keys, block_values, block_index):
        probs = jnp.exp(scores_of(block_keys, block_index) - log_total[..., None])
        key_heads = block_keys.reshape(-1, HEADS, HEAD_DIM)
        value_heads = block_values.reshape(-1, HEADS, HEAD_DIM)
        grad_probs = jnp.einsum(
            "qhd,khd->hqk", grad_heads, value_heads, preferred_element_type=jnp.float32
        )
        grad_scores = (probs * (grad_probs - delta[..., None])).astype(jnp.bfloat16)
        part_query = (
            jnp.einsum("hqk,khd->qhd", grad_scores, key_heads, preferred_element_type=jnp.float32)
            * scale
        )
        part_key = (
            jnp.einsum("hqk,qhd->khd", grad_scores, query_heads, preferred_element_type=jnp.float32)
            * scale
        )
        part_value = jnp.einsum(
            "hqk,qhd->khd",
            probs.astype(jnp.bfloat16),
            grad_heads,
            preferred_element_type=jnp.float32,
        )
        return (part_query, part_key, part_value)

    again = from_behind((keys, values), "rep", 1)
    back_block = (
        jnp.concatenate([again[0], keys], axis=0),
        jnp.concatenate([again[1], values], axis=0),
    )
    query_sum, key_acc, value_acc = block_grads(back_block[0], back_block[1], 0)

    def travel_step(carry, inputs):
        query_total, key_total, value_total, block_keys, block_values = carry
        block_index, kept_keys, kept_values = inputs
        block_keys, block_values = from_behind((block_keys, block_values), "rep", 2)
        key_total, value_total = (
            passed_along(key_total.astype(jnp.bfloat16), "rep", 2).astype(key_total.dtype),
            passed_along(value_total.astype(jnp.bfloat16), "rep", 2).astype(value_total.dtype),
        )
        part_query, part_key, part_value = block_grads(block_keys, block_values, block_index)
        return (
            (
                query_total + part_query,
                key_total + part_key,
                value_total + part_value,
                block_keys,
                block_values,
            ),
            None,
        )

    carry_end, unused_travel = lax.scan(
        travel_step,
        (query_sum, key_acc, value_acc, back_block[0], back_block[1]),
        (block_numbers[1:], key_blocks[1:], value_blocks[1:]),
    )
    query_sum, key_acc, value_acc = (carry_end[0], carry_end[1], carry_end[2])
    from_next = (
        passed_along(key_acc[:tok_dev].astype(jnp.bfloat16), "rep", -1).astype(jnp.float32),
        passed_along(value_acc[:tok_dev].astype(jnp.bfloat16), "rep", -1).astype(jnp.float32),
    )
    joined_key = key_acc[tok_dev:] + from_next[0]
    joined_value = value_acc[tok_dev:] + from_next[1]
    returned = (
        passed_along(joined_key.astype(jnp.bfloat16), "rep", -2 * PAIRS).astype(joined_key.dtype),
        passed_along(joined_value.astype(jnp.bfloat16), "rep", -2 * PAIRS).astype(
            joined_value.dtype
        ),
    )
    grad_query_low = query_sum.reshape(tok_dev, width).astype(jnp.bfloat16)
    grad_key_low = returned[0].reshape(tok_dev, width).astype(jnp.bfloat16)
    grad_value_low = returned[1].reshape(tok_dev, width).astype(jnp.bfloat16)
    grad_w_query = matmul_tn(ln_one, grad_query_low)
    grad_b_query = jnp.sum(grad_query_low.astype(jnp.float32), axis=0)
    grad_w_key = matmul_tn(ln_one, grad_key_low)
    grad_w_value = matmul_tn(ln_one, grad_value_low)
    grad_b_value = jnp.sum(grad_value_low.astype(jnp.float32), axis=0)
    grad_ln_one = (
        matmul_nt(grad_query_low, back_query)
        + matmul_nt(grad_key_low, back_key)
        + matmul_nt(grad_value_low, back_value)
    )
    grad_attn_gain = jnp.sum(grad_ln_one * normed_one, axis=0)
    grad_attn_beta = jnp.sum(grad_ln_one, axis=0)
    grad_input = grad_hidden + norm_grad(
        grad_ln_one, normed_one, inverse_one, back_gain_attn.astype(jnp.float32)
    )
    shares = (
        lax.psum_scatter(
            grad_w_query.astype(jnp.bfloat16), "grp", scatter_dimension=0, tiled=True
        ).astype(jnp.float32),
        lax.psum_scatter(
            grad_w_key.astype(jnp.bfloat16), "grp", scatter_dimension=0, tiled=True
        ).astype(jnp.float32),
        lax.psum_scatter(
            grad_w_value.astype(jnp.bfloat16), "grp", scatter_dimension=0, tiled=True
        ).astype(jnp.float32),
        lax.psum_scatter(
            grad_w_out.astype(jnp.bfloat16), "grp", scatter_dimension=0, tiled=True
        ).astype(jnp.float32),
        lax.psum_scatter(
            grad_w_up.astype(jnp.bfloat16), "grp", scatter_dimension=0, tiled=True
        ).astype(jnp.float32),
        lax.psum_scatter(
            grad_w_down.astype(jnp.bfloat16), "grp", scatter_dimension=0, tiled=True
        ).astype(jnp.float32),
        lax.psum_scatter(
            grad_b_query.astype(jnp.bfloat16), "grp", scatter_dimension=0, tiled=True
        ).astype(jnp.float32),
        lax.psum_scatter(
            grad_b_value.astype(jnp.bfloat16), "grp", scatter_dimension=0, tiled=True
        ).astype(jnp.float32),
        lax.psum_scatter(
            grad_b_out.astype(jnp.bfloat16), "grp", scatter_dimension=0, tiled=True
        ).astype(jnp.float32),
        lax.psum_scatter(
            grad_b_up.astype(jnp.bfloat16), "grp", scatter_dimension=0, tiled=True
        ).astype(jnp.float32),
        lax.psum_scatter(
            grad_b_down.astype(jnp.bfloat16), "grp", scatter_dimension=0, tiled=True
        ).astype(jnp.float32),
        lax.psum_scatter(
            grad_attn_gain.astype(jnp.bfloat16), "grp", scatter_dimension=0, tiled=True
        ).astype(jnp.float32),
        lax.psum_scatter(
            grad_attn_beta.astype(jnp.bfloat16), "grp", scatter_dimension=0, tiled=True
        ).astype(jnp.float32),
        lax.psum_scatter(
            grad_ffn_gain.astype(jnp.bfloat16), "grp", scatter_dimension=0, tiled=True
        ).astype(jnp.float32),
        lax.psum_scatter(
            grad_ffn_beta.astype(jnp.bfloat16), "grp", scatter_dimension=0, tiled=True
        ).astype(jnp.float32),
    )
    totals = (
        lax.psum(shares[0].astype(jnp.bfloat16), "rep").astype(jnp.float32),
        lax.psum(shares[1].astype(jnp.bfloat16), "rep").astype(jnp.float32),
        lax.psum(shares[2].astype(jnp.bfloat16), "rep").astype(jnp.float32),
        lax.psum(shares[3].astype(jnp.bfloat16), "rep").astype(jnp.float32),
        lax.psum(shares[4].astype(jnp.bfloat16), "rep").astype(jnp.float32),
        lax.psum(shares[5].astype(jnp.bfloat16), "rep").astype(jnp.float32),
        lax.psum(shares[6].astype(jnp.bfloat16), "rep").astype(jnp.float32),
        lax.psum(shares[7].astype(jnp.bfloat16), "rep").astype(jnp.float32),
        lax.psum(shares[8].astype(jnp.bfloat16), "rep").astype(jnp.float32),
        lax.psum(shares[9].astype(jnp.bfloat16), "rep").astype(jnp.float32),
        lax.psum(shares[10].astype(jnp.bfloat16), "rep").astype(jnp.float32),
        lax.psum(shares[11].astype(jnp.bfloat16), "rep").astype(jnp.float32),
        lax.psum(shares[12].astype(jnp.bfloat16), "rep").astype(jnp.float32),
        lax.psum(shares[13].astype(jnp.bfloat16), "rep").astype(jnp.float32),
        lax.psum(shares[14].astype(jnp.bfloat16), "rep").astype(jnp.float32),
    )
    return (
        output,
        grad_input,
        totals[0],
        totals[1],
        totals[2],
        totals[3],
        totals[4],
        totals[5],
        totals[6],
        totals[7],
        totals[8],
        totals[9],
        totals[10],
        totals[11],
        totals[12],
        totals[13],
        totals[14],
    )


def solution(mesh):
    in_specs = (
        P(("grp", "rep"), None),
        P("grp", None),
        P("grp", None),
        P("grp", None),
        P("grp", None),
        P("grp", None),
        P("grp", None),
        P("grp", None),
        P("grp"),
        P("grp"),
        P("grp"),
        P("grp"),
        P("grp"),
        P("grp"),
        P("grp"),
        P("grp"),
        P("grp"),
        P(("grp", "rep"), None),
    )
    out_specs = (
        P(("grp", "rep"), None),
        P(("grp", "rep"), None),
        P("grp", None),
        P("grp", None),
        P("grp", None),
        P("grp", None),
        P("grp", None),
        P("grp", None),
        P("grp"),
        P("grp"),
        P("grp"),
        P("grp"),
        P("grp"),
        P("grp"),
        P("grp"),
        P("grp"),
        P("grp"),
    )
    return jax.shard_map(shards, mesh=mesh, in_specs=in_specs, out_specs=out_specs, check_vma=False)
```

profile of v0, /device:TPU:0, one launch (start us, length us, event | category | flops | bytes accessed | tf_op | source)
XLA Modules:
  0.0 1686.0 jit_solution(17164933007839281763)
XLA Ops:
  63.5 43.7 %all-gather.16.cloned.1.call-done = bf16[1280,1280]{1,0:T(8,128)(2,1)} async-done(((bf16[640,1280]{1,0:T(8,128)(2,1)}), bf16[1280,1280]{1,0:T(8,128)(2,1)}) %all-gather.16.cloned.1.call-update) | async-done | bytes 3276816 | tf_op jit(solution)/shard_map/all_gather | solution.py:111
  112.3 42.9 %all-gather.20.cloned.1.call-done = bf16[1280,1280]{1,0:T(8,128)(2,1)} async-done(((bf16[640,1280]{1,0:T(8,128)(2,1)}), bf16[1280,1280]{1,0:T(8,128)(2,1)}) %all-gather.20.cloned.1.call-update) | async-done | bytes 3276816 | tf_op jit(solution)/shard_map/all_gather | solution.py:109
  163.7 132.5 %while.65 = (s32[]{:T(128)}, bf16[256,1280]{1,0:T(8,128)(2,1)S(1)}, bf16[256,1280]{1,0:T(8,128)(2,1)S(1)}, bf16[4,256,1280]{1,2,0:T(8,128)(2,1)}, bf16[4,256,1280]{1,2,0:T(8,128)(2,1)}, /*index=5*/s32[]{:T(128)}) while((s32[]{:T(128)}, bf16[256,1280]{1,0:T(8,128)(2,1)S(1)}, bf16[256,1280]{1,0:T(8,128)(2,1)S(1)}, ...), condition=%wide.region_3.4_spmd, body=%wide.region_2.3_spmd.sunk | while | flops 2 | bytes 13107365 | solution.py:157
  170.5 11.7 collective-permute-done
  182.4 12.7 collective-permute-done.1
  217.0 11.8 collective-permute-done.1
  301.1 19.6 %while.67 = (s32[]{:T(128)}, f32[20,128]{1,0:T(8,128)S(1)}, f32[20,128]{1,0:T(8,128)S(1)}, s32[5]{0:T(128)S(1)}, s32[]{:T(128)}, /*index=5*/s32[3200]{0:T(1024)S...) while((s32[]{:T(128)}, f32[20,128]{1,0:T(8,128)S(1)}, ...), condition=%wide.region_7.8_spmd.clone, body=%wide.region_4.7_spmd.clone.sunk | while | flops 88585096 | bytes 7775018 | solution.py:188
  320.7 25.1 %while.68 = (s32[]{:T(128)}, f32[128,20,64]{0,2,1:T(8,128)}, bf16[5,256,1280]{1,2,0:T(8,128)(2,1)}, s32[5]{0:T(128)S(1)}, s32[]{:T(128)}, /*index=5*/s32[3200]{0...) while((s32[]{:T(128)}, f32[128,20,64]{0,2,1:T(8,128)}, ...), condition=%wide.region_9.10_spmd.clone, body=%wide.region_8.9_spmd.clone.sunk | while | flops 170819984 | bytes 10896233 | solution.py:209
  371.0 151.5 %all-gather.26.cloned.1.call-done = bf16[5120,1280]{1,0:T(8,128)(2,1)} async-done(((bf16[2560,1280]{1,0:T(8,128)(2,1)}), bf16[5120,1280]{1,0:T(8,128)(2,1)}) %all-gather.26.cloned.1.call-update) | async-done | bytes 13107216 | tf_op jit(solution)/shard_map/all_gather | solution.py:114
  551.8 252.9 %while.66 = (s32[]{:T(128)}, f32[128,20,64]{0,2,1:T(8,128)S(1)}, f32[256,20,64]{0,2,1:T(8,128)S(1)}, f32[256,20,64]{0,2,1:T(8,128)}, bf16[256,1280]{0,1:T(8,128)...) while((s32[]{:T(128)}, f32[128,20,64]{0,2,1:T(8,128)S(1)}, ...), condition=%wide.region_16.17_spmd.clone, body=%wide.region_15.16_spmd.clone.sunk | while | flops 428704128 | bytes 45356084 | solution.py:315
  572.1 13.5 collective-permute-done.3
  601.0 11.5 collective-permute-done.5
  636.7 13.5 collective-permute-done.3
  700.5 13.5 collective-permute-done.3
  764.1 13.5 collective-permute-done.3
  822.8 15.4 collective-permute-done.9
  850.4 16.8 collective-permute-done.11
  889.4 14.1 reduce-scatter.13.cloned.1.call-done
  903.5 47.6 %reduce-scatter.9.cloned.1.call-done = bf16[640,1280]{1,0:T(8,128)(2,1)} async-done(((bf16[1280,1280]{1,0:T(8,128)(2,1)}), bf16[640,1280]{1,0:T(8,128)(2,1)}) %reduce-scatter.9.cloned.1.call-update) | async-done | bytes 1638416 | tf_op jit(solution)/shard_map/reduce_scatter | solution.py:355
  951.1 47.6 %reduce-scatter.11.cloned.1.call-done = bf16[640,1280]{1,0:T(8,128)(2,1)} async-done(((bf16[1280,1280]{1,0:T(8,128)(2,1)}), bf16[640,1280]{1,0:T(8,128)(2,1)}) %reduce-scatter.11.cloned.1.call-update) | async-done | bytes 1638416 | tf_op jit(solution)/shard_map/reduce_scatter | solution.py:358
  998.7 153.0 %reduce-scatter.15.cloned.1.call-done = bf16[640,5120]{1,0:T(8,128)(2,1)} async-done(((bf16[1280,5120]{1,0:T(8,128)(2,1)}), bf16[640,5120]{1,0:T(8,128)(2,1)}) %reduce-scatter.15.cloned.1.call-update) | async-done | bytes 6553616 | tf_op jit(solution)/shard_map/reduce_scatter | solution.py:364
  1151.7 152.9 %reduce-scatter.17.cloned.1.call-done = bf16[2560,1280]{1,0:T(8,128)(2,1)} async-done(((bf16[5120,1280]{1,0:T(8,128)(2,1)}), bf16[2560,1280]{1,0:T(8,128)(2,1)}) %reduce-scatter.17.cloned.1.call-update) | async-done | bytes 6553616 | tf_op jit(solution)/shard_map/reduce_scatter | solution.py:367
  1338.1 62.9 %all-reduce.10 = (bf16[640]{0:T(1024)(128)(2,1)S(1)}, bf16[640]{0:T(1024)(128)(2,1)S(1)}, bf16[640]{0:T(1024)(128)(2,1)S(1)}, bf16[2560]{0:T(1024)(128)(2,1)S(1)...) all-reduce(bf16[640]{0:T(1024)(128)(2,1)S(1)} %dynamic-slice.2, ...), channel_id=1, replica_groups=mesh['grp'=2,'rep'=16] {'rep'}, use_global_device_ids=true, to_apply=%region_33.34 | all-reduce | flops 7680 | bytes 30720 | tf_op jit(solution)/shard_map/psum | solution.py:405
  1407.5 247.9 %all-reduce.15.cloned.1.call-done = (bf16[640,1280]{1,0:T(8,128)(2,1)}, bf16[640,1280]{1,0:T(8,128)(2,1)}, bf16[640,1280]{1,0:T(8,128)(2,1)}, bf16[640,1280]{1,0...) async-done(((bf16[640,1280]{1,0:T(8,128)(2,1)}, bf16[640,1280]{1,0:T(8,128)(2,1)}, bf16[640,1280]{1,0:T(8,128)(2,1)}, bf16[640,1280]{1,0:T(8,128)(2,1)}, ...) | async-done | bytes 19660816 | tf_op jit(solution)/shard_map/psum | solution.py:399
  (503 shorter events, 561.1 us)
Async XLA Ops:
  7.2 52.0 %all-gather.18.cloned.1.call-start = ((), (), s32[]{:S(2)}) async-start(), calls=%async_computation.7 | async-start | bytes 4915200 | tf_op jit(solution)/shard_map/all_gather | solution.py:110
  7.9 99.3 %all-gather.16.cloned.1.call-start = ((), (), s32[]{:S(2)}) async-start(), calls=%async_computation.6 | async-start | bytes 4915200 | tf_op jit(solution)/shard_map/all_gather | solution.py:111
  8.7 146.5 %all-gather.20.cloned.1.call-start = ((), (), s32[]{:S(2)}) async-start(), calls=%async_computation.8 | async-start | bytes 4915200 | tf_op jit(solution)/shard_map/all_gather | solution.py:109
  9.4 337.6 %all-gather.22.cloned.1.call-start = ((), (), s32[]{:S(2)}) async-start(), calls=%async_computation.9 | async-start | bytes 4915200 | tf_op jit(solution)/shard_map/all_gather | solution.py:112
  10.0 352.8 %all-gather.24.cloned.1.call-start = ((), (), s32[]{:S(2)}) async-start(), calls=%async_computation.10 | async-start | bytes 19660800 | tf_op jit(solution)/shard_map/all_gather | solution.py:113
  10.7 511.8 %all-gather.26.cloned.1.call-start = ((), (), s32[]{:S(2)}) async-start(), calls=%async_computation.11 | async-start | bytes 19660800 | tf_op jit(solution)/shard_map/all_gather | solution.py:114
  11.3 878.1 %reduce-scatter.7.cloned.1.call-start = ((), (), s32[]{:S(2)}) async-start(), calls=%async_computation.12 | async-start | bytes 4915200 | tf_op jit(solution)/shard_map/reduce_scatter | solution.py:352
  61.8 96.2 %collective-permute-start.7 = (bf16[128,1280]{1,0:T(8,128)(2,1)S(1)}, bf16[128,1280]{1,0:T(8,128)(2,1)S(1)}, u32[]{:S(2)}, u32[]{:S(2)}) collective-permute-start(bf16[128,1280]{1,0:T(8,128)(2,1)S(1)} %convolution_convert_fusion.7), channel_id=1, source_target_pairs={{0,1},{1,2},{2,3},{3,4},{4,5},{5,6},{6,7},{7,8},{8,9},{9,10},{10,1... | collective-permute-start | bytes 983048 | tf_op jit(solution)/shard_map/ppermute | solution.py:20
  109.8 49.5 %collective-permute-start.6 = (bf16[128,1280]{1,0:T(8,128)(2,1)S(1)}, bf16[128,1280]{1,0:T(8,128)(2,1)}, u32[]{:S(2)}, u32[]{:S(2)}) collective-permute-start(bf16[128,1280]{1,0:T(8,128)(2,1)S(1)} %fusion.41), channel_id=1, source_target_pairs={{0,1},{1,2},{2,3},{3,4},{4,5},{5,6},{6,7},{7,8},{8,9},{9,10},{10,1... | collective-permute-start | bytes 983048 | tf_op jit(solution)/shard_map/ppermute | solution.py:20
  561.2 38.4 %collective-permute-start.4 = (bf16[256,20,64]{0,2,1:T(8,128)(2,1)}, bf16[256,20,64]{0,2,1:T(8,128)(2,1)}, u32[]{:S(2)}, u32[]{:S(2)}) collective-permute-start(bf16[256,20,64]{0,2,1:T(8,128)(2,1)} %convert_element_type.454), channel_id=1, source_target_pairs={{14,0},{15,1},{0,2},{1,3},{2,4},{3,5},{4,6},{5,7},{6,8},{7,9},{8,1... | collective-permute-start | bytes 1966088 | tf_op jit(solution)/shard_map/while/body/eval_jaxpr/ppermute | solution.py:26
  562.8 49.7 %collective-permute-start.5 = (bf16[256,20,64]{0,2,1:T(8,128)(2,1)}, bf16[256,20,64]{0,2,1:T(8,128)(2,1)}, u32[]{:S(2)}, u32[]{:S(2)}) collective-permute-start(bf16[256,20,64]{0,2,1:T(8,128)(2,1)} %convert_element_type.455), channel_id=1, source_target_pairs={{14,0},{15,1},{0,2},{1,3},{2,4},{3,5},{4,6},{5,7},{6,8},{7,9},{8,1... | collective-permute-start | bytes 1966088 | tf_op jit(solution)/shard_map/while/body/eval_jaxpr/ppermute | solution.py:26
  626.7 37.5 %collective-permute-start.4 = (bf16[256,20,64]{0,2,1:T(8,128)(2,1)}, bf16[256,20,64]{0,2,1:T(8,128)(2,1)}, u32[]{:S(2)}, u32[]{:S(2)}) collective-permute-start(bf16[256,20,64]{0,2,1:T(8,128)(2,1)} %convert_element_type.454), channel_id=1, source_target_pairs={{14,0},{15,1},{0,2},{1,3},{2,4},{3,5},{4,6},{5,7},{6,8},{7,9},{8,1... | collective-permute-start | bytes 1966088 | tf_op jit(solution)/shard_map/while/body/eval_jaxpr/ppermute | solution.py:26
  627.7 48.6 %collective-permute-start.5 = (bf16[256,20,64]{0,2,1:T(8,128)(2,1)}, bf16[256,20,64]{0,2,1:T(8,128)(2,1)}, u32[]{:S(2)}, u32[]{:S(2)}) collective-permute-start(bf16[256,20,64]{0,2,1:T(8,128)(2,1)} %convert_element_type.455), channel_id=1, source_target_pairs={{14,0},{15,1},{0,2},{1,3},{2,4},{3,5},{4,6},{5,7},{6,8},{7,9},{8,1... | collective-permute-start | bytes 1966088 | tf_op jit(solution)/shard_map/while/body/eval_jaxpr/ppermute | solution.py:26
  691.4 36.6 %collective-permute-start.4 = (bf16[256,20,64]{0,2,1:T(8,128)(2,1)}, bf16[256,20,64]{0,2,1:T(8,128)(2,1)}, u32[]{:S(2)}, u32[]{:S(2)}) collective-permute-start(bf16[256,20,64]{0,2,1:T(8,128)(2,1)} %convert_element_type.454), channel_id=1, source_target_pairs={{14,0},{15,1},{0,2},{1,3},{2,4},{3,5},{4,6},{5,7},{6,8},{7,9},{8,1... | collective-permute-start | bytes 1966088 | tf_op jit(solution)/shard_map/while/body/eval_jaxpr/ppermute | solution.py:26
  692.3 46.7 %collective-permute-start.5 = (bf16[256,20,64]{0,2,1:T(8,128)(2,1)}, bf16[256,20,64]{0,2,1:T(8,128)(2,1)}, u32[]{:S(2)}, u32[]{:S(2)}) collective-permute-start(bf16[256,20,64]{0,2,1:T(8,128)(2,1)} %convert_element_type.455), channel_id=1, source_target_pairs={{14,0},{15,1},{0,2},{1,3},{2,4},{3,5},{4,6},{5,7},{6,8},{7,9},{8,1... | collective-permute-start | bytes 1966088 | tf_op jit(solution)/shard_map/while/body/eval_jaxpr/ppermute | solution.py:26
  748.1 29.5 %collective-permute-start.3 = (bf16[256,1280]{0,1:T(8,128)(2,1)}, bf16[256,1280]{0,1:T(8,128)(2,1)}, u32[]{:S(2)}, u32[]{:S(2)}) collective-permute-start(bf16[256,1280]{0,1:T(8,128)(2,1)} %get-tuple-element.1225), channel_id=1, source_target_pairs={{0,2},{1,3},{2,4},{3,5},{4,6},{5,7},{6,8},{7,9},{8,10},{9,11},{10,... | collective-permute-start | bytes 1966088 | tf_op jit(solution)/shard_map/while/body/eval_jaxpr/ppermute | solution.py:20
  755.1 36.5 %collective-permute-start.4 = (bf16[256,20,64]{0,2,1:T(8,128)(2,1)}, bf16[256,20,64]{0,2,1:T(8,128)(2,1)}, u32[]{:S(2)}, u32[]{:S(2)}) collective-permute-start(bf16[256,20,64]{0,2,1:T(8,128)(2,1)} %convert_element_type.454), channel_id=1, source_target_pairs={{14,0},{15,1},{0,2},{1,3},{2,4},{3,5},{4,6},{5,7},{6,8},{7,9},{8,1... | collective-permute-start | bytes 1966088 | tf_op jit(solution)/shard_map/while/body/eval_jaxpr/ppermute | solution.py:26
  756.0 45.7 %collective-permute-start.5 = (bf16[256,20,64]{0,2,1:T(8,128)(2,1)}, bf16[256,20,64]{0,2,1:T(8,128)(2,1)}, u32[]{:S(2)}, u32[]{:S(2)}) collective-permute-start(bf16[256,20,64]{0,2,1:T(8,128)(2,1)} %convert_element_type.455), channel_id=1, source_target_pairs={{14,0},{15,1},{0,2},{1,3},{2,4},{3,5},{4,6},{5,7},{6,8},{7,9},{8,1... | collective-permute-start | bytes 1966088 | tf_op jit(solution)/shard_map/while/body/eval_jaxpr/ppermute | solution.py:26
  807.9 95.6 %reduce-scatter.13.cloned.1.call-start = ((), (), s32[]{:S(2)}) async-start(), calls=%async_computation.15 | async-start | bytes 4915200 | tf_op jit(solution)/shard_map/reduce_scatter | solution.py:361
  811.7 139.4 %reduce-scatter.9.cloned.1.call-start = ((), (), s32[]{:S(2)}) async-start(), calls=%async_computation.13 | async-start | bytes 4915200 | tf_op jit(solution)/shard_map/reduce_scatter | solution.py:355
  841.9 156.8 %reduce-scatter.11.cloned.1.call-start = ((), (), s32[]{:S(2)}) async-start(), calls=%async_computation.14 | async-start | bytes 4915200 | tf_op jit(solution)/shard_map/reduce_scatter | solution.py:358
  870.0 281.7 %reduce-scatter.15.cloned.1.call-start = ((), (), s32[]{:S(2)}) async-start(), calls=%async_computation.16 | async-start | bytes 19660800 | tf_op jit(solution)/shard_map/reduce_scatter | solution.py:364
  879.3 425.3 %reduce-scatter.17.cloned.1.call-start = ((), (), s32[]{:S(2)}) async-start(), calls=%async_computation.17 | async-start | bytes 19660800 | tf_op jit(solution)/shard_map/reduce_scatter | solution.py:367
  889.3 766.1 %all-reduce.15.cloned.1.call-start = ((), (), s32[]{:S(2)}) async-start(), calls=%async_computation.18 | async-start | bytes 39321600 | tf_op jit(solution)/shard_map/psum | solution.py:399
  (79 other events, 1218.2 us)
Sparse Core Ops, SparseCore 0:
  9.6 49.5 all-gather.17
  60.7 46.4 all-gather.15
  108.7 46.4 all-gather.19
  156.6 46.4 all-gather.21
  204.4 158.2 all-gather.23
  364.2 158.2 all-gather.25
  808.0 47.6 reduce-scatter.6
  858.6 44.7 reduce-scatter.12
  906.3 44.7 reduce-scatter.8
  953.9 44.7 reduce-scatter.10
  1001.5 150.1 reduce-scatter.14
  1154.4 150.1 reduce-scatter.16
  1309.8 345.5 all-reduce.14
where the time goes:
time: 1690 us
  waiting for transfers between devices  1200 us (71%)
  matrix products  134 us (8%)
  blocking collectives  112 us (7%)
  starting transfers between devices  96.5 us (6%)
  local copies, waits for them, and re-layouts  65.3 us (4%)
  other arithmetic  50.3 us (3%)
    psum x1, waiting for transfers between devices, shards(): lax.psum(shares[0].astype(jnp.bfloat16), 'rep').astype(jnp.float32)  248 us
    ppermute x18, waiting for transfers between devices, from_behind(): return lax.ppermute(array, axis, pairs)  161 us
    reduce_scatter x1, waiting for transfers between devices, shards(): lax.psum_scatter(grad_w_up.astype(jnp.bfloat16), 'grp', scatter_dimension...  153 us
    reduce_scatter x1, waiting for transfers between devices, shards(): lax.psum_scatter(grad_w_down.astype(jnp.bfloat16), 'grp', scatter_dimensi...  153 us
    all_gather x1, waiting for transfers between devices, shards(): lax.all_gather(w_down, 'grp', axis=0, tiled=True)  151 us
    ppermute x12, waiting for transfers between devices, passed_along(): return lax.ppermute(block, axis, route)  115 us
    ppermute x18, starting transfers between devices, from_behind(): return lax.ppermute(array, axis, pairs)  78.7 us
    psum x1, blocking collectives, shards(): lax.psum(shares[6].astype(jnp.bfloat16), 'rep').astype(jnp.float32)  62.9 us
  transfers between devices with their start and end apart: 43, of which 39 were waited for; matrix products, arithmetic and copies ran while one was open for 10% of the time, Pallas kernels for 0%

commit v1 on v0

--- a/solution.py
+++ b/solution.py
@@ -1,6 +1,8 @@
 import jax
 import jax.numpy as jnp
 from jax import lax
+from jax.experimental import pallas as pl
+from jax.experimental.pallas import tpu as pltpu
 from jax.sharding import PartitionSpec as P
 
 HEADS = 20
@@ -433,6 +435,308 @@
     )
 
 
+def fits_pair(mesh):
+    return mesh.shape["grp"] == 2 and mesh.shape["rep"] == 16
+
+
+REACH = 9
+CHUNK = 128
+WINDOW = (REACH + 1) * CHUNK
+HALF_LANES = 64
+
+
+def iota(shape, dim):
+    return lax.broadcasted_iota(jnp.int32, shape, dim)
+
+
+def head_half(block, which):
+    first = iota(block.shape, 1) < HALF_LANES
+    return jnp.where(first if which == 0 else jnp.logical_not(first), block, jnp.zeros_like(block))
+
+
+def join_halves(first, second):
+    return jnp.where(iota(first.shape, 1) < HALF_LANES, first, second)
+
+
+def attn_forward(q_ref, k_ref, v_ref, qid_ref, kid_ref, out_ref, lse_ref):
+    span = k_ref.shape[1]
+    query = q_ref[0] * jnp.bfloat16(HEAD_DIM**-0.5)
+    keys, values = k_ref[0], v_ref[0]
+    allowed = (qid_ref[0] == kid_ref[0]) & (
+        iota((CHUNK, span), 1) <= iota((CHUNK, span), 0) + REACH * CHUNK
+    )
+    outs, lses = [], []
+    for which in range(2):
+        scores = jnp.where(allowed, matmul_nt(head_half(query, which), keys), NEGATIVE)
+        top = jnp.max(scores, axis=-1, keepdims=True)
+        probs = jnp.exp(scores - top)
+        total = jnp.sum(probs, axis=-1, keepdims=True)
+        outs.append(matmul((probs * (1.0 / total)).astype(jnp.bfloat16), values))
+        lses.append(jnp.broadcast_to(top + jnp.log(total), (CHUNK, CHUNK)))
+    out_ref[0] = join_halves(*outs)
+    lse_ref[0] = join_halves(*lses)
+
+
+def attn_query_grad(q_ref, k_ref, v_ref, qid_ref, kid_ref, do_ref, out_ref, lse_ref, dq_ref):
+    span = k_ref.shape[1]
+    query = q_ref[0] * jnp.bfloat16(HEAD_DIM**-0.5)
+    keys, values, grad = k_ref[0], v_ref[0], do_ref[0]
+    allowed = (qid_ref[0] == kid_ref[0]) & (
+        iota((CHUNK, span), 1) <= iota((CHUNK, span), 0) + REACH * CHUNK
+    )
+    weighed = grad.astype(jnp.float32) * out_ref[0]
+    parts = []
+    for which in range(2):
+        lse = lse_ref[0][:, which * HALF_LANES : which * HALF_LANES + 1]
+        delta = jnp.sum(head_half(weighed, which), axis=-1, keepdims=True)
+        scores = jnp.where(allowed, matmul_nt(head_half(query, which), keys), NEGATIVE)
+        probs = jnp.exp(scores - lse)
+        grad_probs = matmul_nt(head_half(grad, which), values)
+        grad_scores = (probs * (grad_probs - delta)).astype(jnp.bfloat16)
+        parts.append(matmul(grad_scores, keys))
+    dq_ref[0] = (join_halves(*parts) * HEAD_DIM**-0.5).astype(jnp.bfloat16)
+
+
+def attn_key_grad(k_ref, v_ref, q_ref, do_ref, kid_ref, qid_ref, lse_ref, delta_ref, dk_ref, dv_ref):
+    span = q_ref.shape[1]
+    keys = k_ref[0] * jnp.bfloat16(HEAD_DIM**-0.5)
+    values, queries, grads = v_ref[0], q_ref[0], do_ref[0]
+    allowed = (kid_ref[0] == qid_ref[0]) & (iota((CHUNK, span), 1) >= iota((CHUNK, span), 0))
+    key_parts, value_parts = [], []
+    for which in range(2):
+        scores = jnp.where(allowed, matmul_nt(head_half(keys, which), queries), NEGATIVE)
+        probs = jnp.exp(scores - lse_ref[0, 0, which : which + 1, :])
+        value_parts.append(matmul(probs.astype(jnp.bfloat16), grads))
+        grad_probs = matmul_nt(head_half(values, which), grads)
+        grad_scores = (probs * (grad_probs - delta_ref[0, 0, which : which + 1, :])).astype(
+            jnp.bfloat16
+        )
+        key_parts.append(matmul(grad_scores, queries))
+    dk_ref[0] = (join_halves(*key_parts) * HEAD_DIM**-0.5).astype(jnp.bfloat16)
+    dv_ref[0] = join_halves(*value_parts).astype(jnp.bfloat16)
+
+
+def pair_shards(
+    tokens,
+    doc_ids,
+    w_query,
+    w_key,
+    w_value,
+    w_out,
+    w_up,
+    w_down,
+    b_query,
+    b_value,
+    b_out,
+    b_up,
+    b_down,
+    attn_gain,
+    attn_beta,
+    ffn_gain,
+    ffn_beta,
+    cotangent,
+):
+    f32, bf16 = jnp.float32, jnp.bfloat16
+    chunk, width = tokens.shape
+    half = width // 2
+    row_len = doc_ids.shape[1]
+    side = lax.axis_index("grp")
+    place = lax.axis_index("rep")
+
+    def swap(array):
+        return lax.ppermute(array, "grp", [(0, 1), (1, 0)])
+
+    def cols(array, which, size):
+        return lax.dynamic_slice_in_dim(array, which * size, size, axis=array.ndim - 1)
+
+    def both(own, other, axis):
+        return jnp.where(
+            side == 0,
+            jnp.concatenate([own, other], axis=axis),
+            jnp.concatenate([other, own], axis=axis),
+        )
+
+    small = jnp.concatenate([b_out, b_down, attn_gain, attn_beta, ffn_gain, ffn_beta]).reshape(6, half)
+    small = both(small, swap(small), 1).astype(f32)
+    bias_out, bias_down, gain_one, beta_one, gain_two, beta_two = [small[i] for i in range(6)]
+    ids = jnp.concatenate([doc_ids, swap(doc_ids)], axis=0)
+    moved = swap(jnp.concatenate([tokens, cotangent], axis=0))
+    x_all = jnp.concatenate([tokens, moved[:chunk]], axis=0).astype(f32)
+    cot_all = jnp.concatenate([cotangent, moved[chunk:]], axis=0)
+    w_qkv = jnp.concatenate(
+        [cols(w, side, half) for w in (w_query, w_key, w_value)], axis=1
+    )
+    w_qkv_other = swap(
+        jnp.concatenate([cols(w, 1 - side, half) for w in (w_query, w_key, w_value)], axis=1)
+    )
+    ff_half = w_up.shape[1] // 2
+    w_up_own = cols(w_up, side, ff_half)
+    w_up_other = swap(cols(w_up, 1 - side, ff_half))
+
+    normed_one, inverse_one = norm_rows(x_all)
+    ln_one = (normed_one * gain_one + beta_one).astype(bf16)
+    ln_one_own, ln_one_other = cols(ln_one, side, half), cols(ln_one, 1 - side, half)
+    bias_qkv = jnp.concatenate([b_query.astype(f32), jnp.zeros((half,), f32), b_value.astype(f32)])
+    qkv = (matmul(ln_one_own, w_qkv) + matmul(ln_one_other, w_qkv_other) + bias_qkv).astype(bf16)
+    qkv = qkv.reshape(2, chunk, 3 * half)
+    gathered = lax.all_gather(qkv, "rep", axis=1, tiled=True)
+    front = jnp.pad(gathered[:, :, half:], ((0, 0), (REACH * chunk, 0), (0, 0)))
+    kv_win = lax.dynamic_slice_in_dim(front, place * chunk, WINDOW, axis=1)
+    k_win, v_win = kv_win[:, :, :half], kv_win[:, :, half:]
+    q_own, k_own, v_own = qkv[:, :, :half], qkv[:, :, half : 2 * half], qkv[:, :, 2 * half :]
+    own_ids = lax.dynamic_slice_in_dim(ids, place * chunk, chunk, axis=1)
+    front_ids = jnp.pad(ids, ((0, 0), (REACH * chunk, 0)), constant_values=-1)
+    key_ids = lax.dynamic_slice_in_dim(front_ids, place * chunk, WINDOW, axis=1)
+    back_ids = jnp.pad(ids, ((0, 0), (0, REACH * chunk)), constant_values=-2)
+    query_ids = lax.dynamic_slice_in_dim(back_ids, place * chunk, WINDOW, axis=1)
+
+    pairs = half // CHUNK
+    own_spec = pl.BlockSpec((1, CHUNK, CHUNK), lambda r, p: (r, 0, p))
+    win_spec = pl.BlockSpec((1, WINDOW, CHUNK), lambda r, p: (r, 0, p))
+    col_spec = pl.BlockSpec((1, CHUNK, 1), lambda r, p: (r, 0, 0))
+    row_spec = pl.BlockSpec((1, 1, WINDOW), lambda r, p: (r, 0, 0))
+    stat_spec = pl.BlockSpec((1, 1, 2, WINDOW), lambda r, p: (r, p, 0, 0))
+    own_shape = (2, chunk, half)
+    attn, lse = pl.pallas_call(
+        attn_forward,
+        grid=(2, pairs),
+        in_specs=[own_spec, win_spec, win_spec, col_spec, row_spec],
+        out_specs=[own_spec, own_spec],
+        out_shape=[jax.ShapeDtypeStruct(own_shape, f32)] * 2,
+    )(q_own, k_win, v_win, own_ids[:, :, None], key_ids[:, None, :])
+
+    attn_low = attn.reshape(2 * chunk, half).astype(bf16)
+    mixed = matmul(attn_low, w_out)
+    mixed_other = swap(mixed.astype(bf16)).astype(f32)
+    mixed_other = jnp.concatenate([mixed_other[chunk:], mixed_other[:chunk]], axis=0)
+    hidden = x_all + mixed + mixed_other + bias_out
+    normed_two, inverse_two = norm_rows(hidden)
+    ln_two = (normed_two * gain_two + beta_two).astype(bf16)
+    ln_two_own, ln_two_other = cols(ln_two, side, half), cols(ln_two, 1 - side, half)
+    pre_act = matmul(ln_two_own, w_up_own) + matmul(ln_two_other, w_up_other) + b_up.astype(f32)
+    act_value, act_slope = gelu_pair(pre_act)
+    act_low = act_value.astype(bf16)
+    down = matmul(act_low, w_down)
+    down_other = swap(down[chunk:].astype(bf16)).astype(f32)
+    output = (hidden[:chunk] + down[:chunk] + down_other + bias_down).astype(bf16)
+
+    grad_res = cot_all.astype(f32)
+    grad_w_down = matmul_tn(act_low, cot_all).astype(bf16)
+    grad_pre = (matmul_nt(cot_all, w_down) * act_slope).astype(bf16)
+    grad_up_keep = matmul_tn(ln_two_own, grad_pre).astype(bf16)
+    grad_up_send = matmul_tn(ln_two_other, grad_pre).astype(bf16)
+    back_two = both(matmul_nt(grad_pre, w_up_own), matmul_nt(grad_pre, w_up_other), 1)
+    back_other = swap(back_two.astype(bf16)).astype(f32)
+    grad_ln_two = back_two + jnp.concatenate([back_other[chunk:], back_other[:chunk]], axis=0)
+    grad_hidden = grad_res + norm_grad(grad_ln_two, normed_two, inverse_two, gain_two)
+    grad_mix = grad_hidden.astype(bf16)
+    grad_w_out = matmul_tn(attn_low, grad_mix).astype(bf16)
+    grad_heads = matmul_nt(grad_mix, w_out).astype(bf16)
+
+    delta = jnp.sum(
+        (grad_heads.astype(f32) * attn.reshape(2 * chunk, half)).reshape(2, chunk, half // HEAD_DIM, HEAD_DIM),
+        axis=-1,
+    )
+    stats = jnp.concatenate(
+        [lse.reshape(2, chunk, half // HEAD_DIM, HEAD_DIM)[..., 0], delta], axis=-1
+    )
+    stats = jnp.swapaxes(stats, 1, 2)
+    all_stats = lax.all_gather(stats, "rep", axis=2, tiled=True)
+    all_grads = lax.all_gather(grad_heads.reshape(own_shape), "rep", axis=1, tiled=True)
+    tail = ((0, 0), (0, REACH * chunk), (0, 0))
+    q_win = lax.dynamic_slice_in_dim(jnp.pad(gathered[:, :, :half], tail), place * chunk, WINDOW, axis=1)
+    do_win = lax.dynamic_slice_in_dim(jnp.pad(all_grads, tail), place * chunk, WINDOW, axis=1)
+    stat_win = lax.dynamic_slice_in_dim(
+        jnp.pad(all_stats, ((0, 0), (0, 0), (0, REACH * chunk))), place * chunk, WINDOW, axis=2
+    ).reshape(2, 2, pairs, 2, WINDOW)
+
+    grad_query = pl.pallas_call(
+        attn_query_grad,
+        grid=(2, pairs),
+        in_specs=[own_spec, win_spec, win_spec, col_spec, row_spec, own_spec, own_spec, own_spec],
+        out_specs=own_spec,
+        out_shape=jax.ShapeDtypeStruct(own_shape, bf16),
+    )(
+        q_own,
+        k_win,
+        v_win,
+        own_ids[:, :, None],
+        key_ids[:, None, :],
+        grad_heads.reshape(own_shape),
+        attn,
+        lse,
+    )
+    grad_key, grad_value = pl.pallas_call(
+        attn_key_grad,
+        grid=(2, pairs),
+        in_specs=[own_spec, own_spec, win_spec, win_spec, col_spec, row_spec, stat_spec, stat_spec],
+        out_specs=[own_spec, own_spec],
+        out_shape=[jax.ShapeDtypeStruct(own_shape, bf16)] * 2,
+    )(
+        k_own,
+        v_own,
+        q_win,
+        do_win,
+        own_ids[:, :, None],
+        query_ids[:, None, :],
+        stat_win[:, 0],
+        stat_win[:, 1],
+    )
+    grad_qkv = jnp.concatenate([grad_query, grad_key, grad_value], axis=2).reshape(2 * chunk, 3 * half)
+    grad_qkv_keep = matmul_tn(ln_one_own, grad_qkv).astype(bf16)
+    grad_qkv_send = matmul_tn(ln_one_other, grad_qkv).astype(bf16)
+    back_one = both(matmul_nt(grad_qkv, w_qkv), matmul_nt(grad_qkv, w_qkv_other), 1)
+    back_other = swap(back_one.astype(bf16)).astype(f32)
+    grad_ln_one = back_one + jnp.concatenate([back_other[chunk:], back_other[:chunk]], axis=0)
+    grad_input = grad_hidden + norm_grad(grad_ln_one, normed_one, inverse_one, gain_one)
+
+    def total(array):
+        return jnp.sum(array.astype(f32), axis=0)
+
+    qkv_vec = total(grad_qkv)
+    vectors = [
+        qkv_vec[:half],
+        qkv_vec[2 * half :],
+        cols(total(grad_mix), side, half),
+        total(grad_pre),
+        cols(total(grad_res), side, half),
+        cols(total(grad_ln_one * normed_one), side, half),
+        cols(total(grad_ln_one), side, half),
+        cols(total(grad_ln_two * normed_two), side, half),
+        cols(total(grad_ln_two), side, half),
+    ]
+    vec_sum = lax.psum(jnp.concatenate(vectors).astype(bf16), "rep").astype(f32)
+    cuts, at = [], 0
+    for vector in vectors:
+        cuts.append(vec_sum[at : at + vector.shape[0]])
+        at += vector.shape[0]
+
+    keep_down, keep_out, keep_up, keep_qkv, send_up, send_qkv = [
+        lax.psum_scatter(a, "rep", scatter_dimension=0, tiled=True)
+        for a in (grad_w_down, grad_w_out, grad_up_keep, grad_qkv_keep, grad_up_send, grad_qkv_send)
+    ]
+    other_up, other_qkv = swap(send_up), swap(send_qkv)
+    sum_down, sum_out, sum_up, sum_qkv, sum_up_other, sum_qkv_other = [
+        lax.all_gather(a, "rep", axis=0, tiled=True).astype(f32)
+        for a in (keep_down, keep_out, keep_up, keep_qkv, other_up, other_qkv)
+    ]
+    three = [
+        both(sum_qkv[:, i * half : (i + 1) * half], sum_qkv_other[:, i * half : (i + 1) * half], 1)
+        for i in range(3)
+    ]
+    return (
+        output,
+        grad_input[:chunk],
+        three[0],
+        three[1],
+        three[2],
+        sum_out,
+        both(sum_up, sum_up_other, 1),
+        sum_down,
+        *cuts,
+    )
+
+
 def solution(mesh):
     in_specs = (
         P(("grp", "rep"), None),
@@ -473,4 +777,5 @@
         P("grp"),
         P("grp"),
     )
-    return jax.shard_map(shards, mesh=mesh, in_specs=in_specs, out_specs=out_specs, check_vma=False)
+    plan = pair_shards if fits_pair(mesh) else shards
+    return jax.shard_map(plan, mesh=mesh, in_specs=in_specs, out_specs=out_specs, check_vma=False)

time: 1690 us -> 1090 us (0.64)
  waiting for transfers between devices: 1200 us -> 764 us
  starting transfers between devices: 96.5 us -> 16.2 us
  matrix products: 134 us -> 57.5 us
  Pallas kernels: 0 us -> 39.7 us
  blocking collectives: 112 us -> 81.8 us
    psum x1 -> x0, waiting for transfers between devices: 248 us -> none  [shards(): lax.psum(shares[0].astype(jnp.bfloat16), 'rep').astype(jnp.float32)]
    ppermute x30 -> x11, waiting for transfers between devices: 275 us -> 99.7 us  [swap(): return lax.ppermute(array, 'grp', [(0, 1), (1, 0)])]
    reduce_scatter x6 -> x4, waiting for transfers between devices: 415 us -> 255 us  [pair_shards(): lax.psum_scatter(a, 'rep', scatter_dimension=0, tiled=True)]
    unnamed x13 -> x16, waiting for transfers between devices: 3.75 us -> 127 us
    ppermute x30 -> x11, starting transfers between devices: 96 us -> 15.2 us  [swap(): return lax.ppermute(array, 'grp', [(0, 1), (1, 0)])]
    dot_general x35 -> x0, matrix products: 48.5 us -> none  [the longest x5 13.7 us: block_grads(): jnp.einsum('hqk,qhd->khd', probs.astype(jnp.bfloat16), grad_heads, prefer...]
    pallas_call x0 -> x3, Pallas kernels: none -> 39.7 us  [the longest x1 14.4 us: pair_shards(): pl.pallas_call(attn_forward, grid=(2, pairs), in_specs=[own_spec, win_spe...]
    slice x3 -> x22, local copies, waits for them, and re-layouts: 0.17 us -> 28.3 us  [the longest x1 8.75 us: pair_shards(): front = jnp.pad(gathered[:, :, half:], ((0, 0), (REACH * chunk, 0), (0, 0)))]
  transfers between devices with their start and end apart: 43 -> 25, of which waited for: 39 -> 19; matrix products, arithmetic and copies ran while one was open for 10% -> 12% of each run, Pallas kernels for 0% -> 4%
where the time goes in v1:
time: 1090 us
  waiting for transfers between devices  764 us (70%)
  blocking collectives  81.8 us (8%)
  local copies, waits for them, and re-layouts  57.7 us (5%)
  matrix products  57.5 us (5%)
  other arithmetic  54.4 us (5%)
  Pallas kernels  39.7 us (4%)
  starting transfers between devices  16.2 us (1%)
  between operations  15.2 us (1%)
    reduce_scatter x4, waiting for transfers between devices, pair_shards(): lax.psum_scatter(a, 'rep', scatter_dimension=0, tiled=True)  255 us
    all_gather x6, waiting for transfers between devices, pair_shards(): lax.all_gather(a, 'rep', axis=0, tiled=True).astype(f32)  165 us
    unnamed x16, waiting for transfers between devices  127 us
    all_gather x1, waiting for transfers between devices, pair_shards(): gathered = lax.all_gather(qkv, 'rep', axis=1, tiled=True)  113 us
    ppermute x11, waiting for transfers between devices, swap(): return lax.ppermute(array, 'grp', [(0, 1), (1, 0)])  99.7 us
    psum x1, blocking collectives, pair_shards(): vec_sum = lax.psum(jnp.concatenate(vectors).astype(bf16), 'rep').astype(f32)  60.3 us
    dot_general x6, matrix products, matmul_tn(): lax.dot_general(left, right, (((0,), (0,)), ((), ())), preferred_element_...  23.3 us
  transfers between devices with their start and end apart: 25, of which 19 were waited for; matrix products, arithmetic and copies ran while one was open for 12% of the time, Pallas kernels for 4%

profile of v1, /device:TPU:0, one launch (start us, length us, event | category | flops | bytes accessed | tf_op | source)
XLA Modules:
  0.0 1086.2 jit_solution(7768814377815384793)
XLA Ops:
  23.6 56.6 %collective-permute-done.1 = bf16[6,640]{1,0:T(8,128)(2,1)S(1)} collective-permute-done((bf16[6,640]{1,0:T(8,128)(2,1)S(1)}, bf16[6,640]{1,0:T(8,128)(2,1)S(1)}, u32[]{:S(2)}, u32[]{:S(2)}) %collective-permute-start.1) | collective-permute-done | bytes 7712 | tf_op jit(solution)/shard_map/ppermute | solution.py:547
  96.4 113.3 %all-gather.9.cloned.1.call-done = bf16[2,2048,1920]{2,1,0:T(8,128)(2,1)} async-done(((bf16[2,128,1920]{2,1,0:T(8,128)(2,1)}), bf16[2,2048,1920]{2,1,0:T(8,128)(2,1)}) %all-gather.9.cloned.1.call-update) | async-done | bytes 15728656 | tf_op jit(solution)/shard_map/all_gather | solution.py:582
  209.8 8.7 slice.187
  223.9 14.4 %shard_map.305 = (f32[2,128,640]{2,1,0:T(8,128)}, f32[2,128,640]{2,1,0:T(8,128)}) custom-call(bf16[2,128,640]{2,1,0:T(8,128)(2,1)} %get-tuple-element.64.q_ref, bf16[2,1280,640]{2,1,0:T(8,128)(2,1)} %get-tuple-element.49.k_ref, bf16[2,1280,640]{2,1,0:T(8,128)(2,1)} %get-tuple-element.48.v_ref, s32[2,128,1]{2,1,0:T(8,128)} %copy.43.qid_ref.kid_ref, ...), custom_call_target="tpu_custom_call" | custom-call | tf_op jit(solution)/shard_map/pallas_call | solution.py:600
  242.7 15.6 %collective-permute-done.4 = bf16[256,1280]{1,0:T(8,128)(2,1)S(1)} collective-permute-done((bf16[256,1280]{1,0:T(8,128)(2,1)S(1)}, bf16[256,1280]{1,0:T(8,128)(2,1)S(1)}, u32[]{:S(2)}, u32[]{:S(2)}) %collective-permute-start.4) | collective-permute-done | bytes 655392 | tf_op jit(solution)/shard_map/ppermute | solution.py:547
  278.3 14.9 %collective-permute-done.7 = bf16[256,1280]{1,0:T(8,128)(2,1)S(1)} collective-permute-done((bf16[256,1280]{1,0:T(8,128)(2,1)S(1)}, bf16[256,1280]{1,0:T(8,128)(2,1)S(1)}, u32[]{:S(2)}, u32[]{:S(2)}) %collective-permute-start.7) | collective-permute-done | bytes 655392 | tf_op jit(solution)/shard_map/ppermute | solution.py:547
  315.7 12.1 %shard_map.306 = bf16[2,128,640]{2,1,0:T(8,128)(2,1)} custom-call(bf16[2,128,640]{2,1,0:T(8,128)(2,1)} %get-tuple-element.64.q_ref, bf16[2,1280,640]{2,1,0:T(8,128)(2,1)} %get-tuple-element.49.k_ref, bf16[2,1280,640]{2,1,0:T(8,128)(2,1)} %get-tuple-element.48.v_ref, s32[2,128,1]{2,1,0:T(8,128)} %copy.43.qid_ref.kid_ref, ...), custom_call_target="tpu_custom_call" | custom-call | tf_op jit(solution)/shard_map/pallas_call | solution.py:653
  328.6 21.5 %all_gather.29 = f32[2,20,2048]{2,0,1:T(2,128)S(1)} all-gather(f32[2,20,128]{2,0,1:T(2,128)S(1)} %maximum_bitcast_fusion), channel_id=1, replica_groups=mesh['grp'=2,'rep'=16] {'rep'}, dimensions={2}, use_global_device_ids=true | all-gather | bytes 348160 | tf_op jit(solution)/shard_map/all_gather | solution.py:644
  360.1 13.2 %shard_map.307 = (bf16[2,128,640]{2,1,0:T(8,128)(2,1)}, bf16[2,128,640]{2,1,0:T(8,128)(2,1)}) custom-call(bf16[2,128,640]{2,1,0:T(8,128)(2,1)} %get-tuple-element.63.k_ref, bf16[2,128,640]{2,1,0:T(8,128)(2,1)} %get-tuple-element.62.v_ref, bf16[2,1280,640]{2,1,0:T(8,128)(2,1)} %pad_dynamic-slice_fusion.3.q_ref, ...), custom_call_target="tpu_custom_call" | custom-call | tf_op jit(solution)/shard_map/pallas_call | solution.py:669
  380.6 7.1 convolution_convert_fusion
  387.8 29.6 %reduce-scatter.11.cloned.1.call-done = bf16[40,1280]{1,0:T(8,128)(2,1)} async-done(((bf16[640,1280]{1,0:T(8,128)(2,1)}), bf16[40,1280]{1,0:T(8,128)(2,1)}) %reduce-scatter.11.cloned.1.call-update) | async-done | bytes 102416 | tf_op jit(solution)/shard_map/reduce_scatter | solution.py:715
  417.5 70.6 %reduce-scatter.13.cloned.1.call-done = bf16[40,2560]{1,0:T(8,128)(2,1)} async-done(((bf16[640,2560]{1,0:T(8,128)(2,1)}), bf16[40,2560]{1,0:T(8,128)(2,1)}) %reduce-scatter.13.cloned.1.call-update) | async-done | bytes 204816 | tf_op jit(solution)/shard_map/reduce_scatter | solution.py:715
  488.2 69.8 %reduce-scatter.15.cloned.1.call-done = bf16[40,2560]{1,0:T(8,128)(2,1)} async-done(((bf16[640,2560]{1,0:T(8,128)(2,1)}), bf16[40,2560]{1,0:T(8,128)(2,1)}) %reduce-scatter.15.cloned.1.call-update) | async-done | bytes 204816 | tf_op jit(solution)/shard_map/reduce_scatter | solution.py:715
  564.7 60.0 %reduce-scatter.19.cloned.1.call-done = bf16[40,1920]{1,0:T(8,128)(2,1)} async-done(((bf16[640,1920]{1,0:T(8,128)(2,1)}), bf16[40,1920]{1,0:T(8,128)(2,1)}) %reduce-scatter.19.cloned.1.call-update) | async-done | bytes 153616
  624.8 67.0 %reduce-scatter.21.cloned.1.call-done = bf16[40,1920]{1,0:T(8,128)(2,1)} async-done(((bf16[640,1920]{1,0:T(8,128)(2,1)}), bf16[40,1920]{1,0:T(8,128)(2,1)}) %reduce-scatter.21.cloned.1.call-update) | async-done | bytes 153616
  698.2 84.6 %reduce-scatter.17.cloned.1.call-done = bf16[160,1280]{1,0:T(8,128)(2,1)} async-done(((bf16[2560,1280]{1,0:T(8,128)(2,1)}), bf16[160,1280]{1,0:T(8,128)(2,1)}) %reduce-scatter.17.cloned.1.call-update) | async-done | bytes 409616 | tf_op jit(solution)/shard_map/reduce_scatter | solution.py:715
  782.8 6.1 fusion.51
  800.7 23.2 %all-gather.17.cloned.1.call-done = bf16[640,1280]{1,0:T(8,128)(2,1)} async-done(((bf16[40,1280]{1,0:T(8,128)(2,1)}), bf16[640,1280]{1,0:T(8,128)(2,1)}) %all-gather.17.cloned.1.call-update) | async-done | bytes 1638416 | tf_op jit(solution)/shard_map/all_gather | solution.py:720
  828.4 42.4 %all-gather.19.cloned.1.call-done = bf16[640,2560]{1,0:T(8,128)(2,1)} async-done(((bf16[40,2560]{1,0:T(8,128)(2,1)}), bf16[640,2560]{1,0:T(8,128)(2,1)}) %all-gather.19.cloned.1.call-update) | async-done | bytes 3276816 | tf_op jit(solution)/shard_map/all_gather | solution.py:720
  881.1 60.3 %psum.7 = bf16[7680]{0:T(1024)(128)(2,1)S(1)} all-reduce(bf16[7680]{0:T(1024)(128)(2,1)S(1)} %dynamic-update-slice.8), channel_id=1, replica_groups=mesh['grp'=2,'rep'=16] {'rep'}, use_global_device_ids=true, to_apply=%region_23.24 | all-reduce | flops 7680 | bytes 30720 | tf_op jit(solution)/shard_map/psum | solution.py:708
  947.8 12.2 %maximum_select_fusion = f32[640,5120]{1,0:T(8,128)} fusion(f32[640,2560]{1,0:T(8,128)S(1)} %convert_element_type.159, f32[640,2560]{1,0:T(8,128)} %convert_element_type.157, pred[]{:T(512)S(6)} %eq.2), kind=kLoop, calls=%fused_computation.2 | loop fusion | flops 9830400 | bytes 26214400 | tf_op jit(solution)/shard_map/jit(_where)/select_n | solution.py:553
  965.9 40.0 %all-gather.15.cloned.1.call-done = bf16[640,1920]{1,0:T(8,128)(2,1)} async-done(((bf16[40,1920]{1,0:T(8,128)(2,1)}), bf16[640,1920]{1,0:T(8,128)(2,1)}) %all-gather.15.cloned.1.call-update) | async-done | bytes 2457616 | tf_op jit(solution)/shard_map/all_gather | solution.py:720
  1013.3 57.0 %all-gather.23.cloned.1.call-done = bf16[2560,1280]{1,0:T(8,128)(2,1)} async-done(((bf16[160,1280]{1,0:T(8,128)(2,1)}), bf16[2560,1280]{1,0:T(8,128)(2,1)}) %all-gather.23.cloned.1.call-update) | async-done | bytes 6553616 | tf_op jit(solution)/shard_map/all_gather | solution.py:720
  1070.2 9.0 convert_element_type.161
  (273 shorter events, 161.8 us)
Async XLA Ops:
  7.2 202.6 %all-gather.9.cloned.1.call-start = ((), (), s32[]{:S(2)}) async-start(), calls=%async_computation.6 | async-start | bytes 16711680 | tf_op jit(solution)/shard_map/all_gather | solution.py:582
  9.3 70.9 %collective-permute-start = (bf16[256,1280]{1,0:T(8,128)(2,1)}, bf16[256,1280]{1,0:T(8,128)(2,1)}, u32[]{:S(2)}, u32[]{:S(2)}) collective-permute-start(bf16[256,1280]{1,0:T(8,128)(2,1)} %pad_maximum_fusion.5), channel_id=1, source_target_pairs={{0,16},{16,0},{1,17},{17,1},{2,18},{18,2},{3,19},{19,3},{4,20},{20... | collective-permute-start | bytes 1966088 | tf_op jit(solution)/shard_map/ppermute | solution.py:547
  20.2 64.0 %collective-permute-start.2 = (bf16[640,1920]{1,0:T(8,128)(2,1)}, bf16[640,1920]{1,0:T(8,128)(2,1)}, u32[]{:S(2)}, u32[]{:S(2)}) collective-permute-start(bf16[640,1920]{1,0:T(8,128)(2,1)} %pad_maximum_fusion.1), channel_id=1, source_target_pairs={{0,16},{16,0},{1,17},{17,1},{2,18},{18,2},{3,19},{19,3},{4,20},{20... | collective-permute-start | bytes 7372808 | tf_op jit(solution)/shard_map/ppermute | solution.py:547
  21.5 58.6 %collective-permute-start.1 = (bf16[6,640]{1,0:T(8,128)(2,1)S(1)}, bf16[6,640]{1,0:T(8,128)(2,1)S(1)}, u32[]{:S(2)}, u32[]{:S(2)}) collective-permute-start(bf16[6,640]{1,0:T(8,128)(2,1)S(1)} %reshape.102), channel_id=1, source_target_pairs={{0,16},{16,0},{1,17},{17,1},{2,18},{18,2},{3,19},{19,3},{4,20},{20... | collective-permute-start | bytes 23048 | tf_op jit(solution)/shard_map/ppermute | solution.py:547
  87.8 267.8 %all-gather.11.cloned.1.call-start = ((), (), s32[]{:S(2)}) async-start(), calls=%async_computation.7 | async-start | bytes 5570560 | tf_op jit(solution)/shard_map/all_gather | solution.py:645
  87.9 6.0 collective-permute-start.3
  93.6 170.2 %collective-permute-start.5 = (bf16[640,2560]{1,0:T(8,128)(2,1)}, bf16[640,2560]{1,0:T(8,128)(2,1)}, u32[]{:S(2)}, u32[]{:S(2)}) collective-permute-start(bf16[640,2560]{1,0:T(8,128)(2,1)} %constant_dynamic-slice_fusion), channel_id=1, source_target_pairs={{0,16},{16,0},{1,17},{17,1},{2,18},{18,2},{3,19},{19,3},{4,20},{20... | collective-permute-start | bytes 9830408 | tf_op jit(solution)/shard_map/ppermute | solution.py:547
  241.3 17.1 %collective-permute-start.4 = (bf16[256,1280]{1,0:T(8,128)(2,1)S(1)}, bf16[256,1280]{1,0:T(8,128)(2,1)S(1)}, u32[]{:S(2)}, u32[]{:S(2)}) collective-permute-start(bf16[256,1280]{1,0:T(8,128)(2,1)S(1)} %get-tuple-element.89), channel_id=1, source_target_pairs={{0,16},{16,0},{1,17},{17,1},{2,18},{18,2},{3,19},{19,3},{4,20},{20... | collective-permute-start | bytes 1966088 | tf_op jit(solution)/shard_map/ppermute | solution.py:547
  276.8 16.4 %collective-permute-start.7 = (bf16[256,1280]{1,0:T(8,128)(2,1)S(1)}, bf16[256,1280]{1,0:T(8,128)(2,1)S(1)}, u32[]{:S(2)}, u32[]{:S(2)}) collective-permute-start(bf16[256,1280]{1,0:T(8,128)(2,1)S(1)} %fusion.21), channel_id=1, source_target_pairs={{0,16},{16,0},{1,17},{17,1},{2,18},{18,2},{3,19},{19,3},{4,20},{20... | collective-permute-start | bytes 1966088 | tf_op jit(solution)/shard_map/ppermute | solution.py:547
  296.8 120.6 %reduce-scatter.11.cloned.1.call-start = ((), (), s32[]{:S(2)}) async-start(), calls=%async_computation.10 | async-start | bytes 1740800 | tf_op jit(solution)/shard_map/reduce_scatter | solution.py:715
  300.1 188.0 %reduce-scatter.13.cloned.1.call-start = ((), (), s32[]{:S(2)}) async-start(), calls=%async_computation.12 | async-start | bytes 3481600 | tf_op jit(solution)/shard_map/reduce_scatter | solution.py:715
  304.3 253.7 %reduce-scatter.15.cloned.1.call-start = ((), (), s32[]{:S(2)}) async-start(), calls=%async_computation.14 | async-start | bytes 3481600 | tf_op jit(solution)/shard_map/reduce_scatter | solution.py:715
  308.7 316.0 %reduce-scatter.19.cloned.1.call-start = ((), (), s32[]{:S(2)}) async-start(), calls=%async_computation.18 | async-start | bytes 2611200
  377.1 314.6 %reduce-scatter.21.cloned.1.call-start = ((), (), s32[]{:S(2)}) async-start(), calls=%async_computation.19 | async-start | bytes 2611200
  379.5 403.2 %reduce-scatter.17.cloned.1.call-start = ((), (), s32[]{:S(2)}) async-start(), calls=%async_computation.16 | async-start | bytes 6963200 | tf_op jit(solution)/shard_map/reduce_scatter | solution.py:715
  387.7 436.2 %all-gather.17.cloned.1.call-start = ((), (), s32[]{:S(2)}) async-start(), calls=%async_computation.11 | async-start | bytes 1740800 | tf_op jit(solution)/shard_map/all_gather | solution.py:720
  417.4 453.3 %all-gather.19.cloned.1.call-start = ((), (), s32[]{:S(2)}) async-start(), calls=%async_computation.13 | async-start | bytes 3481600 | tf_op jit(solution)/shard_map/all_gather | solution.py:720
  488.1 456.8 %all-gather.21.cloned.1.call-start = ((), (), s32[]{:S(2)}) async-start(), calls=%async_computation.15 | async-start | bytes 3481600 | tf_op jit(solution)/shard_map/all_gather | solution.py:720
  558.0 6.0 collective-permute-start.10
  564.7 397.6 %all-gather.13.cloned.1.call-start = ((), (), s32[]{:S(2)}) async-start(), calls=%async_computation.8 | async-start | bytes 2611200 | tf_op jit(solution)/shard_map/all_gather | solution.py:720
  624.8 381.1 %all-gather.15.cloned.1.call-start = ((), (), s32[]{:S(2)}) async-start(), calls=%async_computation.9 | async-start | bytes 2611200 | tf_op jit(solution)/shard_map/all_gather | solution.py:720
  697.9 372.4 %all-gather.23.cloned.1.call-start = ((), (), s32[]{:S(2)}) async-start(), calls=%async_computation.17 | async-start | bytes 6963200 | tf_op jit(solution)/shard_map/all_gather | solution.py:720
  789.0 10.5 collective-permute-start.6
  794.7 81.7 %collective-permute-start.8 = (bf16[256,1280]{1,0:T(8,128)(2,1)S(1)}, bf16[256,1280]{1,0:T(8,128)(2,1)}, u32[]{:S(2)}, u32[]{:S(2)}) collective-permute-start(bf16[256,1280]{1,0:T(8,128)(2,1)S(1)} %fusion.20), channel_id=1, source_target_pairs={{0,16},{16,0},{1,17},{17,1},{2,18},{18,2},{3,19},{19,3},{4,20},{20... | collective-permute-start | bytes 1966088 | tf_op jit(solution)/shard_map/ppermute | solution.py:547
  (54 other events, 550.3 us)
Sparse Core Ops, SparseCore 0:
  87.9 121.7 all-gather.8
  296.9 58.6 all-gather.10
  359.3 58.0 reduce-scatter.10
  422.1 65.9 reduce-scatter.12
  492.3 65.6 reduce-scatter.14
  562.8 61.9 reduce-scatter.18
  629.6 62.0 reduce-scatter.20
  696.8 85.8 reduce-scatter.16
  784.9 38.9 all-gather.16
  826.0 44.6 all-gather.18
  873.6 44.9 all-gather.20
  920.6 41.6 all-gather.12
  964.4 41.4 all-gather.14
  1008.0 62.1 all-gather.22

commit v2 on v1

--- a/solution.py
+++ b/solution.py
@@ -516,6 +516,365 @@
     dv_ref[0] = join_halves(*value_parts).astype(jnp.bfloat16)
 
 
+MESH_ID = pl.DeviceIdType.MESH
+RING = 8
+SHARD = 240
+PARTS = ((0, 128), (128, 112))
+UP_CUT = 160
+QKV_CUT = 176
+
+
+def device_at(side, level, column, core):
+    return (side, (level * 2 + column) * 2 + core)
+
+
+def ring_device(side, spot, core):
+    level = jnp.where(spot < 4, spot, 7 - spot)
+    return device_at(side, level, spot // 4, core)
+
+
+def greet(partners):
+    barrier = pltpu.get_barrier_semaphore()
+    for partner in partners:
+        pl.semaphore_signal(barrier, inc=1, device_id=partner, device_id_type=MESH_ID)
+    pl.semaphore_wait(barrier, len(partners))
+
+
+def sum_kernel(
+    in_ref,
+    vec_ref,
+    out_ref,
+    vec_out_ref,
+    mine,
+    theirs,
+    landed,
+    swapped,
+    vec_steps,
+    vec_landed,
+    load_sem,
+    core_sems,
+    ring_sems,
+    back_sems,
+    share_sems,
+    swap_sems,
+    vec_sems,
+    keep_sem,
+):
+    side = lax.axis_index("grp")
+    place = lax.axis_index("rep")
+    level, column, core = place // 4, (place // 2) % 2, place % 2
+    spot = jnp.where(column == 0, level, 7 - level)
+    sibling = device_at(side, level, column, 1 - core)
+    across = device_at(1 - side, level, column, core)
+    ahead = ring_device(side, (spot + 1) % RING, core)
+    behind = ring_device(side, (spot + RING - 1) % RING, core)
+    near = level + 1 - 2 * (level % 2)
+    far = (level + 2) % 4
+    vec_partners = (
+        sibling,
+        device_at(side, level, 1 - column, core),
+        device_at(side, near, column, core),
+        device_at(side, far, column, core),
+    )
+    greet((ahead, behind, across) + vec_partners)
+    targets = (ahead, behind)
+
+    def remote(source, target, sems, where, device):
+        return pltpu.make_async_remote_copy(
+            source,
+            target,
+            sems.at[(0,) + where],
+            sems.at[(1,) + where],
+            device_id=device,
+            device_id_type=MESH_ID,
+        )
+
+    def shard_at(way, offset):
+        return (spot + RING + (1 - 2 * way) * offset) % RING
+
+    def load(way, shard):
+        return pltpu.make_async_copy(
+            in_ref.at[core, way, shard], mine.at[way, shard], load_sem.at[way, shard]
+        )
+
+    def cross(way, shard):
+        return remote(
+            in_ref.at[1 - core, way, shard],
+            theirs.at[way, shard],
+            core_sems,
+            (way, shard),
+            sibling,
+        )
+
+    def start_inputs(step, unused):
+        for way in range(2):
+            shard = shard_at(way, RING - 1 - step)
+            load(way, shard).start()
+            cross(way, shard).start()
+        return unused
+
+    lax.fori_loop(0, RING, start_inputs, 0)
+
+    vec_steps[0] = vec_ref[...]
+    vec_copy = [
+        remote(vec_steps.at[k], vec_landed.at[k], vec_sems, (k,), vec_partners[k])
+        for k in range(4)
+    ]
+    vec_copy[0].start()
+
+    def ring_copy(way, part, step):
+        first, rows = PARTS[part]
+        shard = shard_at(way, RING - 1 - step)
+        return remote(
+            mine.at[way, shard, pl.ds(first, rows)],
+            landed.at[way, step, pl.ds(first, rows)],
+            ring_sems,
+            (way, part, step),
+            targets[way],
+        )
+
+    def add_inputs(way, part, shard, step):
+        first, rows = PARTS[part]
+        here = pl.ds(first, rows)
+        value = mine[way, shard, here, :].astype(jnp.float32) + theirs[
+            way, shard, here, :
+        ].astype(jnp.float32)
+        if step is not None:
+            value = value + landed[way, step, here, :].astype(jnp.float32)
+        mine[way, shard, here, :] = value.astype(jnp.bfloat16)
+
+    for way in range(2):
+        shard = shard_at(way, RING - 1)
+        load(way, shard).wait()
+        cross(way, shard).wait()
+    for part in range(2):
+        for way in range(2):
+            add_inputs(way, part, shard_at(way, RING - 1), None)
+            ring_copy(way, part, 0).start()
+    for k in range(4):
+        vec_copy[k].wait()
+        vec_steps[k + 1] = vec_steps[k] + vec_landed[k]
+        if k < 3:
+            vec_copy[k + 1].start()
+    vec_out_ref[...] = vec_steps[4]
+
+    def ring_step(step, unused):
+        for way in range(2):
+            shard = shard_at(way, RING - 1 - step)
+            load(way, shard).wait()
+            cross(way, shard).wait()
+        for part in range(2):
+            for way in range(2):
+                ring_copy(way, part, step - 1).wait()
+                add_inputs(way, part, shard_at(way, RING - 1 - step), step - 1)
+                ring_copy(way, part, step).start()
+        return unused
+
+    lax.fori_loop(1, RING - 1, ring_step, 0)
+    for way in range(2):
+        load(way, spot).wait()
+        cross(way, spot).wait()
+
+    def back_copy(way, part, step):
+        first, rows = PARTS[part]
+        here = pl.ds(first, rows)
+        shard = shard_at(way, RING - step)
+        source = mine if isinstance(step, int) and step == 0 else out_ref.at[core]
+        return remote(
+            source.at[way, shard, here],
+            out_ref.at[core, way, shard, here],
+            back_sems,
+            (way, part, step),
+            targets[way],
+        )
+
+    def share(way, part, step):
+        first, rows = PARTS[part]
+        here = pl.ds(first, rows)
+        shard = shard_at(way, RING - step)
+        source = mine if isinstance(step, int) and step == 0 else out_ref.at[core]
+        return remote(
+            source.at[way, shard, here],
+            out_ref.at[core, way, shard, here],
+            share_sems,
+            (way, part, step),
+            sibling,
+        )
+
+    def keep(way, part):
+        first, rows = PARTS[part]
+        here = pl.ds(first, rows)
+        return pltpu.make_async_copy(
+            mine.at[way, spot, here], out_ref.at[core, way, spot, here], keep_sem.at[way, part]
+        )
+
+    def publish(way, part):
+        back_copy(way, part, 0).start()
+        share(way, part, 0).start()
+        keep(way, part).start()
+
+    last = RING - 2
+    swaps = (pl.ds(UP_CUT, SHARD - UP_CUT), pl.ds(QKV_CUT, SHARD - QKV_CUT))
+    trades = core * RING + spot < 2 * RING - 1
+
+    def swap_copy(way):
+        return remote(
+            mine.at[way, spot, swaps[way]],
+            swapped.at[way, pl.ds(0, SHARD - (UP_CUT, QKV_CUT)[way])],
+            swap_sems,
+            (way,),
+            across,
+        )
+
+    for way in range(2):
+        ring_copy(way, 0, last).wait()
+        add_inputs(way, 0, spot, last)
+        publish(way, 0)
+    for way in range(2):
+        ring_copy(way, 1, last).wait()
+        add_inputs(way, 1, spot, last)
+        if way == 0:
+            swap_copy(0).start()
+        else:
+
+            @pl.when(trades)
+            def _():
+                swap_copy(1).start()
+
+    swap_copy(0).wait()
+    mine[0, spot, swaps[0], :] = swapped[0]
+    publish(0, 1)
+
+    @pl.when(trades)
+    def _():
+        swap_copy(1).wait()
+        mine[1, spot, swaps[1], :] = swapped[1, : SHARD - QKV_CUT, :]
+
+    publish(1, 1)
+
+    for part in range(2):
+        for way in range(2):
+            back_copy(way, part, 0).wait()
+            back_copy(way, part, jnp.int32(1)).start()
+            share(way, part, jnp.int32(1)).start()
+
+    def back_step(step, unused):
+        for part in range(2):
+            for way in range(2):
+                back_copy(way, part, step).wait()
+                back_copy(way, part, step + 1).start()
+                share(way, part, step + 1).start()
+        return unused
+
+    lax.fori_loop(1, last, back_step, 0)
+    for part in range(2):
+        for way in range(2):
+            back_copy(way, part, jnp.int32(last)).wait()
+            share(way, part, jnp.int32(RING - 1)).start()
+            keep(way, part).wait()
+            share(way, part, 0).wait()
+
+    def share_end(step, unused):
+        for part in range(2):
+            for way in range(2):
+                share(way, part, step).wait()
+        return unused
+
+    lax.fori_loop(1, RING, share_end, 0)
+
+
+def sum_over_rep(buffer, vectors, number):
+    dma = pltpu.SemaphoreType.DMA
+    return pl.pallas_call(
+        sum_kernel,
+        out_shape=[
+            jax.ShapeDtypeStruct(buffer.shape, jnp.bfloat16),
+            jax.ShapeDtypeStruct(vectors.shape, jnp.float32),
+        ],
+        in_specs=[
+            pl.BlockSpec(memory_space=pl.ANY),
+            pl.BlockSpec(memory_space=pltpu.VMEM),
+        ],
+        out_specs=[
+            pl.BlockSpec(memory_space=pl.ANY),
+            pl.BlockSpec(memory_space=pltpu.VMEM),
+        ],
+        scratch_shapes=[
+            pltpu.VMEM((2, RING, SHARD, 1280), jnp.bfloat16),
+            pltpu.VMEM((2, RING, SHARD, 1280), jnp.bfloat16),
+            pltpu.VMEM((2, RING - 1, SHARD, 1280), jnp.bfloat16),
+            pltpu.VMEM((2, SHARD - UP_CUT, 1280), jnp.bfloat16),
+            pltpu.VMEM((5,) + vectors.shape, jnp.float32),
+            pltpu.VMEM((4,) + vectors.shape, jnp.float32),
+            dma((2, RING)),
+            dma((2, 2, RING)),
+            dma((2, 2, 2, RING - 1)),
+            dma((2, 2, 2, RING - 1)),
+            dma((2, 2, 2, RING)),
+            dma((2, 2)),
+            dma((2, 4)),
+            dma((2, 2)),
+        ],
+        compiler_params=pltpu.CompilerParams(
+            collective_id=number, has_side_effects=True, vmem_limit_bytes=56 * 2**20
+        ),
+    )(buffer, vectors)
+
+
+def tall(array):
+    blocks = [array[:, i : i + 1280] for i in range(0, array.shape[1] - 1279, 1280)]
+    if array.shape[1] % 1280:
+        rest = array[:, -640:]
+        blocks.append(jnp.concatenate([rest[:320], rest[320:]], axis=1))
+    return jnp.concatenate(blocks, axis=0)
+
+
+def wide(array):
+    blocks = [array[i : i + 640] for i in range(0, array.shape[0] - 639, 640)]
+    if array.shape[0] % 640:
+        rest = array[-320:]
+        blocks.append(jnp.concatenate([rest[:, :640], rest[:, 640:]], axis=0))
+    return jnp.concatenate(blocks, axis=1)
+
+
+def pack_shards(down, out, up_keep, up_send, qkv_keep, qkv_send):
+    count = 2 * RING
+    first = jnp.concatenate(
+        [down.reshape(count, UP_CUT, -1), tall(up_send).reshape(count, SHARD - UP_CUT, -1)],
+        axis=1,
+    )
+    keep = jnp.concatenate([out, tall(up_keep), tall(qkv_keep)], axis=0)
+    send = tall(qkv_send)
+    edge = (count - 1) * QKV_CUT
+    second = jnp.concatenate(
+        [
+            jnp.concatenate(
+                [
+                    keep[:edge].reshape(count - 1, QKV_CUT, -1),
+                    send.reshape(count - 1, SHARD - QKV_CUT, -1),
+                ],
+                axis=1,
+            ),
+            keep[edge:][None],
+        ],
+        axis=0,
+    )
+    shape = (2, RING, SHARD, down.shape[1])
+    return jnp.stack([first.reshape(shape), second.reshape(shape)], axis=1)
+
+
+def unpack_shards(sums):
+    count = 2 * RING
+    width = sums.shape[-1]
+    first = sums[:, 0].reshape(count, SHARD, width)
+    second = sums[:, 1].reshape(count, SHARD, width)
+    down = first[:, :UP_CUT].reshape(-1, width)
+    up_send = wide(first[:, UP_CUT:].reshape(-1, width))
+    keep = jnp.concatenate([second[:-1, :QKV_CUT].reshape(-1, width), second[-1]], axis=0)
+    qkv_send = wide(second[:-1, QKV_CUT:].reshape(-1, width))
+    return (down, keep[:640], wide(keep[640:1920]), up_send, wide(keep[1920:]), qkv_send)
+
+
 def pair_shards(
     tokens,
     doc_ids,
@@ -705,21 +1064,21 @@
         cols(total(grad_ln_two * normed_two), side, half),
         cols(total(grad_ln_two), side, half),
     ]
-    vec_sum = lax.psum(jnp.concatenate(vectors).astype(bf16), "rep").astype(f32)
+    packed = jnp.concatenate(vectors)
+    lanes = 128
+    packed = jnp.pad(packed, (0, 64 * lanes - packed.shape[0])).reshape(64, lanes)
+    buffer = pack_shards(
+        grad_w_down, grad_w_out, grad_up_keep, grad_up_send, grad_qkv_keep, grad_qkv_send
+    )
+    sums, vec_sum = sum_over_rep(buffer, packed, 1)
+    vec_sum = vec_sum.reshape(-1)
     cuts, at = [], 0
     for vector in vectors:
         cuts.append(vec_sum[at : at + vector.shape[0]])
         at += vector.shape[0]
-
-    keep_down, keep_out, keep_up, keep_qkv, send_up, send_qkv = [
-        lax.psum_scatter(a, "rep", scatter_dimension=0, tiled=True)
-        for a in (grad_w_down, grad_w_out, grad_up_keep, grad_qkv_keep, grad_up_send, grad_qkv_send)
-    ]
-    other_up, other_qkv = swap(send_up), swap(send_qkv)
-    sum_down, sum_out, sum_up, sum_qkv, sum_up_other, sum_qkv_other = [
-        lax.all_gather(a, "rep", axis=0, tiled=True).astype(f32)
-        for a in (keep_down, keep_out, keep_up, keep_qkv, other_up, other_qkv)
-    ]
+    sum_down, sum_out, sum_up, sum_up_other, sum_qkv, sum_qkv_other = unpack_shards(
+        sums.astype(f32)
+    )
     three = [
         both(sum_qkv[:, i * half : (i + 1) * half], sum_qkv_other[:, i * half : (i + 1) * half], 1)
         for i in range(3)

time: 1090 us -> 721 us (0.66)
  waiting for transfers between devices: 764 us -> 201 us
  Pallas kernels: 39.7 us -> 241 us
  local copies, waits for them, and re-layouts: 57.7 us -> 132 us
  blocking collectives: 81.8 us -> 21.4 us
    reduce_scatter x4 -> x0, waiting for transfers between devices: 255 us -> none  [pair_shards(): lax.psum_scatter(a, 'rep', scatter_dimension=0, tiled=True)]
    pallas_call x0 -> x1, Pallas kernels: none -> 201 us  [sum_over_rep(): pl.pallas_call(sum_kernel, out_shape=[jax.ShapeDtypeStruct(buffer.shape,...]
    all_gather x6 -> x0, waiting for transfers between devices: 165 us -> none  [pair_shards(): lax.all_gather(a, 'rep', axis=0, tiled=True).astype(f32)]
    unnamed x16 -> x2, waiting for transfers between devices: 127 us -> 0.03 us
    psum x1 -> x0, blocking collectives: 60.3 us -> none  [pair_shards(): vec_sum = lax.psum(jnp.concatenate(vectors).astype(bf16), 'rep').astype(f32)]
    slice x1 -> x13, local copies, waits for them, and re-layouts: 0.01 us -> 59.4 us  [the longest x3 16.2 us: wide(): blocks = [array[i:i + 640] for i in range(0, array.shape[0] - 639, 640)]]
    convert_element_type x4 -> x0, other arithmetic: 20.7 us -> none  [pair_shards(): lax.all_gather(a, 'rep', axis=0, tiled=True).astype(f32)]
    unnamed x119 -> x156, local copies, waits for them, and re-layouts: 7.84 us -> 22.6 us
  transfers between devices with their start and end apart: 25 -> 11, of which waited for: 19 -> 4; matrix products, arithmetic and copies ran while one was open for 12% -> 12% of each run, Pallas kernels for 4% -> 4%
where the time goes in v2:
time: 721 us; the launch traced here: 716 us
  Pallas kernels  241 us (33%)
  waiting for transfers between devices  201 us (28%)
  local copies, waits for them, and re-layouts  132 us (18%)
  matrix products  48 us (7%)
  other arithmetic  44.4 us (6%)
  blocking collectives  21.4 us (3%)
  between operations  15.3 us (2%)
  starting transfers between devices  12.3 us (2%)
    pallas_call x1, Pallas kernels, sum_over_rep(): pl.pallas_call(sum_kernel, out_shape=[jax.ShapeDtypeStruct(buffer.shape,...  201 us
    all_gather x1, waiting for transfers between devices, pair_shards(): gathered = lax.all_gather(qkv, 'rep', axis=1, tiled=True)  113 us
    ppermute x9, waiting for transfers between devices, swap(): return lax.ppermute(array, 'grp', [(0, 1), (1, 0)])  88 us
    unnamed x156, local copies, waits for them, and re-layouts  22.6 us
    all_gather x1, blocking collectives, pair_shards(): all_stats = lax.all_gather(stats, 'rep', axis=2, tiled=True)  21.4 us
    dot_general x6, matrix products, matmul(): return jnp.dot(left, right, preferred_element_type=jnp.float32)  18.5 us
    dot_general x6, matrix products, matmul_nt(): lax.dot_general(left, right, (((1,), (1,)), ((), ())), preferred_element_...  16.5 us
    slice x3, local copies, waits for them, and re-layouts, wide(): blocks = [array[i:i + 640] for i in range(0, array.shape[0] - 639, 640)]  16.2 us
  transfers between devices with their start and end apart: 11, of which 4 were waited for; matrix products, arithmetic and copies ran while one was open for 12% of the time, Pallas kernels for 4%

profile of v2, /device:TPU:0, one launch (start us, length us, event | category | flops | bytes accessed | tf_op | source)
XLA Modules:
  0.0 715.5 jit_solution(16251926265798678240)
XLA Ops:
  22.8 57.4 %collective-permute-done.1 = bf16[6,640]{1,0:T(8,128)(2,1)S(1)} collective-permute-done((bf16[6,640]{1,0:T(8,128)(2,1)S(1)}, bf16[6,640]{1,0:T(8,128)(2,1)S(1)}, u32[]{:S(2)}, u32[]{:S(2)}) %collective-permute-start.1) | collective-permute-done | bytes 7712 | tf_op jit(solution)/shard_map/ppermute | solution.py:906
  90.0 3.9 constant_dynamic-slice_fusion
  96.8 113.1 %all-gather.3.cloned.1.call-done = bf16[2,2048,1920]{2,1,0:T(8,128)(2,1)} async-done(((bf16[2,128,1920]{2,1,0:T(8,128)(2,1)}), bf16[2,2048,1920]{2,1,0:T(8,128)(2,1)}) %all-gather.3.cloned.1.call-update) | async-done | bytes 15728656 | tf_op jit(solution)/shard_map/all_gather | solution.py:941
  209.8 8.7 %slice.367 = bf16[2,2048,1280]{2,1,0:T(8,128)(2,1)} slice(bf16[2,2048,1920]{2,1,0:T(8,128)(2,1)} %all-gather.3.cloned.1.call-done), slice={[0:2], [0:2048], [640:1920]} | slice | bytes 20971520 | tf_op jit(solution)/shard_map/slice | solution.py:942
  218.6 5.4 pad_dynamic-slice_fusion.1
  224.0 14.3 %shard_map.305 = (f32[2,128,640]{2,1,0:T(8,128)}, f32[2,128,640]{2,1,0:T(8,128)}) custom-call(bf16[2,128,640]{2,1,0:T(8,128)(2,1)} %get-tuple-element.83.q_ref, bf16[2,1280,640]{2,1,0:T(8,128)(2,1)} %get-tuple-element.64.k_ref, bf16[2,1280,640]{2,1,0:T(8,128)(2,1)} %get-tuple-element.63.v_ref, s32[2,128,1]{2,1,0:T(8,128)} %copy.35.qid_ref.kid_ref, ...), custom_call_target="tpu_custom_call" | custom-call | tf_op jit(solution)/shard_map/pallas_call | solution.py:959
  243.4 15.6 %collective-permute-done.4 = bf16[256,1280]{1,0:T(8,128)(2,1)S(1)} collective-permute-done((bf16[256,1280]{1,0:T(8,128)(2,1)S(1)}, bf16[256,1280]{1,0:T(8,128)(2,1)S(1)}, u32[]{:S(2)}, u32[]{:S(2)}) %collective-permute-start.4) | collective-permute-done | bytes 655392 | tf_op jit(solution)/shard_map/ppermute | solution.py:906
  268.0 5.4 convert_reduce_fusion
  279.4 14.9 %collective-permute-done.7 = bf16[256,1280]{1,0:T(8,128)(2,1)S(1)} collective-permute-done((bf16[256,1280]{1,0:T(8,128)(2,1)S(1)}, bf16[256,1280]{1,0:T(8,128)(2,1)S(1)}, u32[]{:S(2)}, u32[]{:S(2)}) %collective-permute-start.7) | collective-permute-done | bytes 655392 | tf_op jit(solution)/shard_map/ppermute | solution.py:906
  306.1 5.4 fusion.55
  314.2 5.4 convolution_convert_fusion
  325.5 12.2 %shard_map.306 = bf16[2,128,640]{2,1,0:T(8,128)(2,1)} custom-call(bf16[2,128,640]{2,1,0:T(8,128)(2,1)} %get-tuple-element.83.q_ref, bf16[2,1280,640]{2,1,0:T(8,128)(2,1)} %get-tuple-element.64.k_ref, bf16[2,1280,640]{2,1,0:T(8,128)(2,1)} %get-tuple-element.63.v_ref, s32[2,128,1]{2,1,0:T(8,128)} %copy.35.qid_ref.kid_ref, ...), custom_call_target="tpu_custom_call" | custom-call | tf_op jit(solution)/shard_map/pallas_call | solution.py:1012
  338.5 21.4 %all_gather.11 = f32[2,20,2048]{2,0,1:T(2,128)S(1)} all-gather(f32[2,20,128]{2,0,1:T(2,128)S(1)} %maximum_bitcast_fusion), channel_id=1, replica_groups=mesh['grp'=2,'rep'=16] {'rep'}, dimensions={2}, use_global_device_ids=true | all-gather | bytes 348160 | tf_op jit(solution)/shard_map/all_gather | solution.py:1003
  365.8 4.6 pad_dynamic-slice_fusion.2.do_ref
  370.4 13.3 %shard_map.307 = (bf16[2,128,640]{2,1,0:T(8,128)(2,1)}, bf16[2,128,640]{2,1,0:T(8,128)(2,1)}) custom-call(bf16[2,128,640]{2,1,0:T(8,128)(2,1)} %get-tuple-element.82.k_ref, bf16[2,128,640]{2,1,0:T(8,128)(2,1)} %get-tuple-element.81.v_ref, bf16[2,1280,640]{2,1,0:T(8,128)(2,1)} %pad_dynamic-slice_fusion.3.q_ref, ...), custom_call_target="tpu_custom_call" | custom-call | tf_op jit(solution)/shard_map/pallas_call | solution.py:1028
  403.9 8.5 %pad_maximum_fusion.in_ref = bf16[2,2,8,240,1280]{4,3,2,1,0:T(8,128)(2,1)} fusion(bf16[2,1,8,240,1280]{4,3,2,1,0:T(8,128)(2,1)S(1)} %bitcast.87, bf16[2,1,8,80,1280]{4,3,2,1,0:T(8,128)(2,1)S(1)} %bitcast.89, bf16[2,1,8,160,1280]{4,3,2,1,0:T(8,128)(2,1)S(1)} %bitcast.103), kind=kLoop, calls=%fused_computation | loop fusion | flops 58982400 | bytes 39321600 | tf_op jit(solution)/shard_map/stack | solution.py:863
  416.4 201.4 %shard_map.308 = (bf16[2,2,8,240,1280]{4,3,2,1,0:T(8,128)(2,1)}, f32[64,128]{1,0:T(8,128)}) custom-call(bf16[2,2,8,240,1280]{4,3,2,1,0:T(8,128)(2,1)} %pad_maximum_fusion.in_ref, f32[64,128]{1,0:T(8,128)} %pad_bitcast_fusion.vec_ref), custom_call_target="tpu_custom_call" | custom-call | tf_op jit(solution)/shard_map/pallas_call | solution.py:788
  620.5 16.0 %fusion.61 = (f32[2,1,8,240,1280]{4,3,2,1,0:T(8,128)}, f32[2,1,8,240,1280]{4,3,2,1,0:T(8,128)S(1)}) fusion(bf16[2,2,8,240,1280]{4,3,2,1,0:T(8,128)(2,1)} %get-tuple-element.27), kind=kLoop, calls=%fused_computation.181 | loop fusion | bytes 78643200 | tf_op jit(solution)/shard_map/slice | solution.py:869
  639.6 4.5 copy-done.2
  646.1 10.6 %slice.410 = f32[15,176,1280]{2,1,0:T(8,128)} slice(f32[16,240,1280]{2,1,0:T(8,128)} %bitcast.86), slice={[0:15], [0:176], [0:1280]} | slice | bytes 27033600 | tf_op jit(solution)/shard_map/slice | solution.py:873
  659.9 7.9 %fusion.62 = (f32[640,1280]{1,0:T(8,128)}, f32[640,1280]{1,0:T(8,128)}, f32[640,1280]{1,0:T(8,128)}) fusion(f32[2640,1280]{1,0:T(8,128)} %bitcast.79), kind=kLoop, calls=%fused_computation.182 | loop fusion | bytes 19660800 | tf_op jit(solution)/shard_map/slice | solution.py:833
  667.9 6.2 fusion.60
  674.1 11.0 %slice.426 = f32[16,160,1280]{2,1,0:T(8,128)} slice(f32[16,240,1280]{2,1,0:T(8,128)} %bitcast.82), slice={[0:16], [0:160], [0:1280]} | slice | bytes 26214400 | tf_op jit(solution)/shard_map/slice | solution.py:871
  700.6 5.7 maximum_select_fusion
  (283 shorter events, 127.3 us)
Async XLA Ops:
  7.2 233.0 %copy-start = (bf16[640,1280]{1,0:T(8,128)(2,1)S(1)}, bf16[640,1280]{1,0:T(8,128)(2,1)}, u32[]{:S(2)}) copy-start(bf16[640,1280]{1,0:T(8,128)(2,1)} %param.23) | copy-start | bytes 4915204
  7.2 202.6 %all-gather.3.cloned.1.call-start = ((), (), s32[]{:S(2)}) async-start(), calls=%async_computation | async-start | bytes 16711680 | tf_op jit(solution)/shard_map/all_gather | solution.py:941
  9.4 70.9 %collective-permute-start = (bf16[256,1280]{1,0:T(8,128)(2,1)}, bf16[256,1280]{1,0:T(8,128)(2,1)}, u32[]{:S(2)}, u32[]{:S(2)}) collective-permute-start(bf16[256,1280]{1,0:T(8,128)(2,1)} %pad_maximum_fusion.11), channel_id=1, source_target_pairs={{0,16},{16,0},{1,17},{17,1},{2,18},{18,2},{3,19},{19,3},{4,20},{20... | collective-permute-start | bytes 1966088 | tf_op jit(solution)/shard_map/ppermute | solution.py:906
  17.7 64.4 %copy-start.5 = (bf16[128,1280]{1,0:T(8,128)(2,1)S(1)}, bf16[128,1280]{1,0:T(8,128)(2,1)}, u32[]{:S(2)}) copy-start(bf16[128,1280]{1,0:T(8,128)(2,1)} %param.18) | copy-start | bytes 983044
  19.4 63.8 %copy-start.46 = (bf16[640,640]{1,0:T(8,128)(2,1)S(1)}, bf16[640,640]{1,0:T(8,128)(2,1)}, u32[]{:S(2)}) copy-start(bf16[640,640]{1,0:T(8,128)(2,1)} %get-tuple-element.76) | copy-start | bytes 2457604
  19.4 64.8 %collective-permute-start.2 = (bf16[640,1920]{1,0:T(8,128)(2,1)}, bf16[640,1920]{1,0:T(8,128)(2,1)}, u32[]{:S(2)}, u32[]{:S(2)}) collective-permute-start(bf16[640,1920]{1,0:T(8,128)(2,1)} %pad_maximum_fusion.4), channel_id=1, source_target_pairs={{0,16},{16,0},{1,17},{17,1},{2,18},{18,2},{3,19},{19,3},{4,20},{20... | collective-permute-start | bytes 7372808 | tf_op jit(solution)/shard_map/ppermute | solution.py:906
  20.7 59.5 %collective-permute-start.1 = (bf16[6,640]{1,0:T(8,128)(2,1)S(1)}, bf16[6,640]{1,0:T(8,128)(2,1)S(1)}, u32[]{:S(2)}, u32[]{:S(2)}) collective-permute-start(bf16[6,640]{1,0:T(8,128)(2,1)S(1)} %reshape.139), channel_id=1, source_target_pairs={{0,16},{16,0},{1,17},{17,1},{2,18},{18,2},{3,19},{19,3},{4,20},{20... | collective-permute-start | bytes 23048 | tf_op jit(solution)/shard_map/ppermute | solution.py:906
  22.7 60.4 %copy-start.48 = (bf16[640,640]{1,0:T(8,128)(2,1)S(1)}, bf16[640,640]{1,0:T(8,128)(2,1)}, u32[]{:S(2)}) copy-start(bf16[640,640]{1,0:T(8,128)(2,1)} %get-tuple-element.78) | copy-start | bytes 2457604
  22.8 60.4 %copy-start.49 = (bf16[640,640]{1,0:T(8,128)(2,1)S(1)}, bf16[640,640]{1,0:T(8,128)(2,1)}, u32[]{:S(2)}) copy-start(bf16[640,640]{1,0:T(8,128)(2,1)} %get-tuple-element.80) | copy-start | bytes 2457604
  82.6 602.5 %copy-start.53 = (f32[256]{0:T(256)}, f32[256]{0:T(256)S(1)}, u32[]{:S(2)}) copy-start(f32[256]{0:T(256)S(1)} %add_rsqrt_fusion.1) | copy-start | bytes 3076
  87.9 277.9 %all-gather.5.cloned.1.call-start = ((), (), s32[]{:S(2)}) async-start(), calls=%async_computation.1 | async-start | bytes 5570560 | tf_op jit(solution)/shard_map/all_gather | solution.py:1004
  88.2 6.0 collective-permute-start.3
  93.9 170.6 %collective-permute-start.5 = (bf16[640,2560]{1,0:T(8,128)(2,1)}, bf16[640,2560]{1,0:T(8,128)(2,1)}, u32[]{:S(2)}, u32[]{:S(2)}) collective-permute-start(bf16[640,2560]{1,0:T(8,128)(2,1)} %constant_dynamic-slice_fusion), channel_id=1, source_target_pairs={{0,16},{16,0},{1,17},{17,1},{2,18},{18,2},{3,19},{19,3},{4,20},{20... | collective-permute-start | bytes 9830408 | tf_op jit(solution)/shard_map/ppermute | solution.py:906
  241.9 17.1 %collective-permute-start.4 = (bf16[256,1280]{1,0:T(8,128)(2,1)S(1)}, bf16[256,1280]{1,0:T(8,128)(2,1)S(1)}, u32[]{:S(2)}, u32[]{:S(2)}) collective-permute-start(bf16[256,1280]{1,0:T(8,128)(2,1)S(1)} %get-tuple-element.106), channel_id=1, source_target_pairs={{0,16},{16,0},{1,17},{17,1},{2,18},{18,2},{3,19},{19,3},{4,20},{20... | collective-permute-start | bytes 1966088 | tf_op jit(solution)/shard_map/ppermute | solution.py:906
  243.4 15.7 %copy-start.23 = (f32[256,1280]{1,0:T(8,128)S(1)}, f32[256,1280]{1,0:T(8,128)}, u32[]{:S(2)}) copy-start(f32[256,1280]{1,0:T(8,128)} %get-tuple-element.107) | copy-start | bytes 3932164
  277.9 16.4 %collective-permute-start.7 = (bf16[256,1280]{1,0:T(8,128)(2,1)S(1)}, bf16[256,1280]{1,0:T(8,128)(2,1)S(1)}, u32[]{:S(2)}, u32[]{:S(2)}) collective-permute-start(bf16[256,1280]{1,0:T(8,128)(2,1)S(1)} %fusion.23), channel_id=1, source_target_pairs={{0,16},{16,0},{1,17},{17,1},{2,18},{18,2},{3,19},{19,3},{4,20},{20... | collective-permute-start | bytes 1966088 | tf_op jit(solution)/shard_map/ppermute | solution.py:906
  311.6 13.1 %collective-permute-start.6 = (bf16[128,1280]{1,0:T(8,128)(2,1)S(1)}, bf16[128,1280]{1,0:T(8,128)(2,1)S(1)}, u32[]{:S(2)}, u32[]{:S(2)}) collective-permute-start(bf16[128,1280]{1,0:T(8,128)(2,1)S(1)} %slice.476), channel_id=1, source_target_pairs={{0,16},{16,0},{1,17},{17,1},{2,18},{18,2},{3,19},{19,3},{4,20},{20... | collective-permute-start | bytes 983048 | tf_op jit(solution)/shard_map/ppermute | solution.py:906
  325.5 12.2 %copy-start.36 = (f32[256,640]{1,0:T(8,128)S(1)}, f32[256,640]{1,0:T(8,128)}, u32[]{:S(2)}) copy-start(f32[256,640]{1,0:T(8,128)} %get-tuple-element.108) | copy-start | bytes 1966084
  337.7 23.8 %copy-start.9 = (f32[256,1280]{1,0:T(8,128)S(1)}, f32[256,1280]{1,0:T(8,128)}, u32[]{:S(2)}) copy-start(f32[256,1280]{1,0:T(8,128)} %copy-done.8) | copy-start | bytes 3932164
  337.7 23.7 %copy-start.31 = (bf16[256,640]{1,0:T(8,128)(2,1)S(1)}, bf16[256,640]{1,0:T(8,128)(2,1)}, u32[]{:S(2)}) copy-start(bf16[256,640]{1,0:T(8,128)(2,1)} %copy-done.30) | copy-start | bytes 983044
  338.5 24.8 %copy-start.3 = (bf16[640,2560]{1,0:T(8,128)(2,1)S(1)}, bf16[640,2560]{1,0:T(8,128)(2,1)}, u32[]{:S(2)}) copy-start(bf16[640,2560]{1,0:T(8,128)(2,1)} %convolution_convert_fusion.1) | copy-start | bytes 9830404
  370.4 13.4 %copy-start.41 = (bf16[2,128,640]{2,1,0:T(8,128)(2,1)S(1)}, bf16[2,128,640]{2,1,0:T(8,128)(2,1)}, u32[]{:S(2)}) copy-start(bf16[2,128,640]{2,1,0:T(8,128)(2,1)} %shard_map.306) | copy-start | bytes 983044
  370.4 14.6 %copy-start.47 = (bf16[640,640]{1,0:T(8,128)(2,1)S(1)}, bf16[640,640]{1,0:T(8,128)(2,1)}, u32[]{:S(2)}) copy-start(bf16[640,640]{1,0:T(8,128)(2,1)} %get-tuple-element.76) | copy-start | bytes 2457604
  393.6 19.1 %collective-permute-start.8 = (bf16[256,1280]{1,0:T(8,128)(2,1)}, bf16[256,1280]{1,0:T(8,128)(2,1)}, u32[]{:S(2)}, u32[]{:S(2)}) collective-permute-start(bf16[256,1280]{1,0:T(8,128)(2,1)} %fusion.22), channel_id=1, source_target_pairs={{0,16},{16,0},{1,17},{17,1},{2,18},{18,2},{3,19},{19,3},{4,20},{20... | collective-permute-start | bytes 1966088 | tf_op jit(solution)/shard_map/ppermute | solution.py:906
  (59 other events, 226.8 us)
Sparse Core Ops, SparseCore 0:
  88.0 121.7 all-gather.2
  298.6 56.8 all-gather.4

commit v3 on v0

--- a/solution.py
+++ b/solution.py
@@ -1,6 +1,8 @@
 import jax
 import jax.numpy as jnp
 from jax import lax
+from jax.experimental import pallas as pl
+from jax.experimental.pallas import tpu as pltpu
 from jax.sharding import PartitionSpec as P
 
 HEADS = 20
@@ -433,6 +435,1511 @@
     )
 
 
+def fits_pair(mesh):
+    return mesh.shape["grp"] == 2 and mesh.shape["rep"] == 16
+
+
+REACH = 9
+CHUNK = 128
+WINDOW = (REACH + 1) * CHUNK
+HALF_LANES = 64
+
+
+def iota(shape, dim):
+    return lax.broadcasted_iota(jnp.int32, shape, dim)
+
+
+def head_half(block, which):
+    first = iota(block.shape, 1) < HALF_LANES
+    return jnp.where(first if which == 0 else jnp.logical_not(first), block, jnp.zeros_like(block))
+
+
+def join_halves(first, second):
+    return jnp.where(iota(first.shape, 1) < HALF_LANES, first, second)
+
+
+SLOTS = 12
+LEVELS = 4
+
+
+class Stream:
+    def __init__(self, side, spot, mirrored, view, sems):
+        self.side, self.mirrored, self.view, self.sems = side, mirrored, view, sems
+        level, column, core = spot
+        if mirrored:
+            level, column, core = LEVELS - 1 - level, 1 - column, 1 - core
+        self.level, self.column, self.core = level, column, core
+
+    def device(self, level, column, core):
+        if self.mirrored:
+            level, column, core = LEVELS - 1 - level, 1 - column, 1 - core
+        return device_at(self.side, level, column, core)
+
+    def slot(self, holder, chunk):
+        gaps = [c - h for c, h in zip(chunk, holder)]
+        return SLOTS - 1 + 4 * gaps[0] + 2 * gaps[1] + gaps[2]
+
+    def copy(self, kind, chunk, target):
+        me = (self.level, self.column, self.core)
+        return remote(
+            self.view(self.slot(me, chunk)),
+            self.view(self.slot(target, chunk)),
+            self.sems,
+            (kind,),
+            self.device(*target),
+        )
+
+    def arrived(self, kind):
+        here = self.view(SLOTS - 1)
+        twin = self.device(self.level, self.column, 1 - self.core)
+        remote(here, here, self.sems, (kind,), twin).wait_recv()
+
+    def up(self, back):
+        chunk = (self.level - back, self.column, self.core)
+        target = ((self.level + 1) % LEVELS, self.column, self.core)
+        if back == 2:
+            chunk, target = (self.level - 1, 1, 1), ((self.level + 2) % LEVELS, 0, 0)
+        return self.copy(back, chunk, target)
+
+    def over(self, back):
+        chunk = (self.level - back, self.column, self.core)
+        return self.copy(3 + back, chunk, (self.level, 1 - self.column, self.core))
+
+    def twin(self, back):
+        chunk = (self.level - back, self.column, self.core)
+        return self.copy(6 + back, chunk, (self.level, self.column, 1 - self.core))
+
+    def pass_on(self, back):
+        chunk = (self.level - back, 1 - self.column, self.core)
+        return self.copy(9 + back, chunk, (self.level, self.column, 1 - self.core))
+
+    def sends_up(self, back):
+        if back == 2:
+            return (self.level == LEVELS - 3) & (self.column == 0) & (self.core == 1)
+        return (self.level >= back) & (self.level < LEVELS - 1)
+
+    def gets_up(self, back):
+        if back == 2:
+            return (self.level == LEVELS - 1) & (self.column + self.core == 0)
+        return self.level >= back + 1
+
+    def sends_over(self, back):
+        if back == 0:
+            return self.column == 0
+        if back == 1:
+            return self.level >= 1
+        return (self.level >= 2) & (self.column + self.core >= 1)
+
+    def gets_over(self, back):
+        if back == 0:
+            return self.column == 1
+        if back == 1:
+            return self.level >= 1
+        return (self.level >= 2) & (1 - self.column + self.core >= 1)
+
+    def sends_twin(self, back):
+        return self.core == 0 if back == 0 else self.level >= back
+
+    def gets_twin(self, back):
+        return self.core == 1 if back == 0 else self.level >= back
+
+    def gets_pass(self, back):
+        if back < 2:
+            return self.gets_over(back)
+        return (self.level >= 2) & (2 - self.column - self.core >= 1)
+
+    def start_own(self, wide=True):
+        pl.when(self.sends_up(0))(lambda: self.up(0).start())
+        pl.when(self.sends_twin(0))(lambda: self.twin(0).start())
+        self.start_over(0, wide)
+
+    def start_over(self, back, wide=True):
+        pl.when(self.sends_over(back) & wide)(lambda: self.over(back).start())
+
+    def after_up(self, back, wide=True):
+        @pl.when(self.gets_up(back))
+        def _():
+            self.arrived(back)
+
+        if back == 0:
+            pl.when(self.sends_up(1))(lambda: self.up(1).start())
+        self.start_over(back + 1, wide)
+        pl.when(self.sends_twin(back + 1))(lambda: self.twin(back + 1).start())
+
+    def after_over(self, back):
+        @pl.when(self.gets_over(back))
+        def _():
+            self.arrived(3 + back)
+            self.pass_on(back).start()
+
+        if back == 1:
+            pl.when(self.sends_up(2))(lambda: self.up(2).start())
+
+    def after_twins(self):
+        for back in range(3):
+            pl.when(self.gets_twin(back))(lambda: self.arrived(6 + back))
+            pl.when(self.gets_pass(back))(lambda: self.arrived(9 + back))
+        pl.when(self.gets_up(2))(lambda: self.arrived(2))
+
+    def finish(self):
+        for back in range(3):
+            pl.when(self.sends_up(back))(lambda: self.up(back).wait_send())
+            pl.when(self.sends_over(back))(lambda: self.over(back).wait_send())
+            pl.when(self.sends_twin(back))(lambda: self.twin(back).wait_send())
+            pl.when(self.gets_over(back))(lambda: self.pass_on(back).wait_send())
+
+
+def spot_of(place):
+    return (place // 4, (place // 2) % 2, place % 2)
+
+
+def neighbours(side, spot):
+    level, column, core = spot
+    return (
+        device_at(1 - side, level, column, core),
+        device_at(side, level, column, 1 - core),
+        device_at(side, level, 1 - column, core),
+        device_at(side, (level + 1) % LEVELS, column, core),
+        device_at(side, (level + LEVELS - 1) % LEVELS, column, core),
+    )
+
+
+def rows_of(ref):
+    return lambda slot: ref.at[:, tile(CHUNK * slot, CHUNK, CHUNK), :]
+
+
+def row_of(ref, row):
+    return lambda slot: ref.at[row, tile(CHUNK * slot, CHUNK, CHUNK), :]
+
+
+def far_corners(side, spot):
+    level, column, core = spot
+    return (device_at(side, (level + 2) % LEVELS, column, 1 - core),)
+
+
+def front_kernel(
+    tok_ref,
+    cot_ref,
+    ids_ref,
+    small_ref,
+    wk_ref,
+    wv_ref,
+    wq_ref,
+    wup_ref,
+    w_out_ref,
+    kwin_out,
+    vwin_out,
+    qwin_out,
+    k_own,
+    v_own,
+    q_own,
+    ln_out,
+    tok_other,
+    cot_other,
+    ids_other,
+    small_all,
+    w_other_out,
+    wup_other,
+    attn_ref,
+    lse_ref,
+    mixed_ref,
+    ids_all,
+    kwin,
+    vwin,
+    qwin,
+    w_other,
+    w_own,
+    ln_all,
+    sent,
+    came,
+    own_sem,
+    y_sems,
+    w_sems,
+    flow_sems,
+    mix_sems,
+    out_sem,
+):
+    side = lax.axis_index("grp")
+    spot = spot_of(lax.axis_index("rep"))
+    level, column, core = spot
+    across, twin, over, above, below = neighbours(side, spot)
+    near = device_at(side, level + 1 - 2 * (level % 2), column, core)
+    f32, bf16 = jnp.float32, jnp.bfloat16
+    half = w_own.shape[1]
+    for win in (kwin, vwin, qwin):
+        win[...] = jnp.zeros_like(win)
+    greet((across, twin, over, above, below) + far_corners(side, spot))
+
+    weights = (wk_ref, wv_ref, wq_ref)
+    quarter = half // 4
+
+    def part(owner):
+        return tile(quarter * owner, quarter)
+
+    mine = 2 * (level % 2) + core
+    own_cols, other_cols = tile(half * side, half, 128), tile(half * (1 - side), half, 128)
+    y_small = remote(small_ref, small_all.at[:, own_cols], y_sems, (0,), across)
+    y_ids = remote(ids_ref, ids_other, y_sems, (1,), across)
+    y_tok = remote(tok_ref, tok_other, y_sems, (2,), across)
+    y_cot = remote(cot_ref, cot_other, y_sems, (3,), across)
+    ff_half = wup_other.shape[1]
+
+    def w_part(m, owner):
+        return wup_other.at[part(owner)] if m == 3 else w_other.at[m, part(owner)]
+
+    def w_across(m):
+        if m == 3:
+            source = wup_ref.at[part(mine), tile(ff_half * (1 - side), ff_half, 128)]
+        else:
+            source = weights[m].at[part(mine), other_cols]
+        return remote(source, w_part(m, mine), w_sems, (0, m), across)
+
+    def w_over(m):
+        here = w_part(m, mine)
+        return remote(here, here, w_sems, (1, m), near)
+
+    def w_twin(m):
+        here = w_part(m, mine)
+        return remote(here, here, w_sems, (2, m), twin)
+
+    def w_pass(m):
+        here = w_part(m, 2 * (1 - level % 2) + core)
+        return remote(here, here, w_sems, (3, m), twin)
+
+    def w_load(m):
+        return pltpu.make_async_copy(weights[m].at[:, own_cols], w_own.at[m], own_sem.at[m])
+
+    y_small.start()
+    w_across(0).start()
+    w_across(1).start()
+    for m in range(3):
+        w_load(m).start()
+
+    small_all[:, own_cols] = small_ref[...]
+
+    def norm_into(rows, ref):
+        x = ref[...].astype(f32)
+        center = x - jnp.mean(x, axis=-1, keepdims=True)
+        inverse = lax.rsqrt(jnp.mean(center * center, axis=-1, keepdims=True) + EPSILON)
+        gain, beta = small_all[2:3, :].astype(f32), small_all[3:4, :].astype(f32)
+        ln_all[rows, :] = (center * inverse * gain + beta).astype(bf16)
+        ln_out[rows, :half] = ln_all[rows, own_cols]
+        ln_out[rows, half:] = ln_all[rows, other_cols]
+
+    def w_forward(m):
+        w_across(m).wait_recv()
+        w_over(m).start()
+        w_twin(m).start()
+
+    def w_second(m):
+        w_over(m).wait_recv()
+        w_pass(m).start()
+
+    wins, biases = (kwin, vwin, qwin), (None, 7, 6)
+
+    def project(m, row):
+        rows = pl.ds(CHUNK * row, CHUNK)
+        value = matmul(ln_out[rows, :half], w_own[m]) + matmul(ln_out[rows, half:], w_other[m])
+        if biases[m] is not None:
+            value = value + small_ref[biases[m] : biases[m] + 1, :].astype(f32)
+        wins[m][row, pl.ds((SLOTS - 1) * CHUNK, CHUNK), :] = value.astype(bf16)
+        (k_own, v_own, q_own)[m][rows, :] = value.astype(bf16)
+
+    def win_out(m, row):
+        target = (kwin_out, vwin_out, qwin_out)[m]
+        return pltpu.make_async_copy(wins[m].at[row], target.at[row], out_sem.at[m, row])
+
+    w_out_copy = pltpu.make_async_copy(w_other, w_other_out, out_sem.at[3, 0])
+
+    def w_ready(m):
+        w_load(m).wait()
+        w_twin(m).wait_recv()
+        w_pass(m).wait_recv()
+
+    flows = [
+        [
+            Stream(side, spot, m == 2, row_of(wins[m], row), flow_sems.at[3 * row + m])
+            for m in range(3)
+        ]
+        for row in range(2)
+    ]
+    pairs_of = [flow[:2] for flow in flows]
+    queries = [flow[2] for flow in flows]
+
+    def each(streams, event, *args):
+        for stream in streams:
+            getattr(stream, event)(*args)
+
+    w_forward(0)
+    y_ids.start()
+    y_small.wait()
+    y_tok.start()
+    norm_into(pl.ds(0, CHUNK), tok_ref)
+    w_forward(1)
+    w_across(2).start()
+    w_second(0)
+    w_ready(0)
+    project(0, 0)
+    flows[0][0].start_own()
+    w_second(1)
+    w_ready(1)
+    project(1, 0)
+    flows[0][1].start_own()
+    y_tok.wait_recv()
+    norm_into(pl.ds(CHUNK, CHUNK), tok_other)
+    project(0, 1)
+    flows[1][0].start_own()
+    project(1, 1)
+    flows[1][1].start_own()
+    each(pairs_of[0], "after_up", 0)
+    w_forward(2)
+    w_across(3).start()
+    y_cot.start()
+    each(pairs_of[0], "after_over", 0)
+    w_second(2)
+    each(pairs_of[1], "after_up", 0)
+    w_ready(2)
+    project(2, 0)
+    project(2, 1)
+    light = level < 2
+    each(queries, "start_own", light)
+    w_out_copy.start()
+    each(pairs_of[0], "after_up", 1)
+    each(pairs_of[1], "after_over", 0)
+    each(pairs_of[1], "after_up", 1)
+    each(pairs_of[0], "after_over", 1)
+    each(queries, "after_up", 0, light)
+    w_forward(3)
+    each(pairs_of[0], "after_over", 2)
+    each(pairs_of[1], "after_over", 1)
+    each(queries, "after_up", 1, light)
+    for back in range(3):
+        each(queries, "start_over", back, jnp.logical_not(light))
+    y_ids.wait()
+    place = lax.axis_index("rep")
+    ids_all[:, : REACH * CHUNK] = jnp.full((8, REACH * CHUNK), -1, jnp.int32)
+    row_end = REACH * CHUNK + ids_ref.shape[1]
+    ids_all[:, row_end:] = jnp.full((8, REACH * CHUNK), -2, jnp.int32)
+    ids_all[:, REACH * CHUNK : row_end] = jnp.zeros((8, ids_ref.shape[1]), jnp.int32)
+    ids_all[0:1, REACH * CHUNK : row_end] = ids_ref[...]
+    ids_all[1:2, REACH * CHUNK : row_end] = ids_other[...]
+    each(pairs_of[0], "after_twins")
+    win_out(0, 0).start()
+    win_out(1, 0).start()
+    pairs = half // CHUNK
+    window = pl.ds((SLOTS - 1 - REACH) * CHUNK, WINDOW)
+    own_slot = pl.ds((SLOTS - 1) * CHUNK, CHUNK)
+    upper, lower = pl.ds(0, CHUNK), pl.ds(CHUNK, CHUNK)
+    mix_copy = (
+        remote(sent.at[upper], came.at[lower], mix_sems, (0,), across),
+        remote(sent.at[lower], came.at[upper], mix_sems, (1,), across),
+    )
+
+    def mix(row):
+        rows = pl.ds(CHUNK * row, CHUNK)
+        mixed = matmul(attn_ref[rows, :].astype(bf16), w_out_ref[...])
+        mixed_ref[rows, :] = mixed
+        sent[rows, :] = mixed.astype(bf16)
+        mix_copy[row].start()
+
+    def unit(i, unused):
+        row, block = i // pairs, i % pairs
+        rows, lanes = tile(CHUNK * row, CHUNK, CHUNK), tile(CHUNK * block, CHUNK, CHUNK)
+        query = qwin[row, own_slot, lanes] * jnp.bfloat16(HEAD_DIM**-0.5)
+        key_block, value_block = kwin[row, window, lanes], vwin[row, window, lanes]
+        key_ids = ids_all[:2, tile(CHUNK * place, WINDOW, CHUNK)].astype(f32)
+        key_ids = jnp.where(row == 0, key_ids[0:1], key_ids[1:2])
+        query_ids = jnp.broadcast_to(key_ids[:, -CHUNK:], (CHUNK, CHUNK)).T[:, :1]
+        allowed = (query_ids == key_ids) & (
+            iota((CHUNK, WINDOW), 1) <= iota((CHUNK, WINDOW), 0) + REACH * CHUNK
+        )
+        outs, lses = [], []
+        for which in range(2):
+            scores = jnp.where(allowed, matmul_nt(head_half(query, which), key_block), NEGATIVE)
+            top = jnp.max(scores, axis=-1, keepdims=True)
+            probs = jnp.exp(scores - top)
+            total = jnp.sum(probs, axis=-1, keepdims=True)
+            outs.append(matmul((probs * (1.0 / total)).astype(bf16), value_block))
+            lses.append(jnp.broadcast_to(top + jnp.log(total), (CHUNK, CHUNK)))
+        attn_ref[rows, lanes] = join_halves(*outs)
+        lse_ref[rows, lanes] = join_halves(*lses)
+        pl.when(i == 2)(lambda: each(pairs_of[1], "after_over", 2))
+        return unused
+
+    lax.fori_loop(0, pairs, unit, 0)
+    mix(0)
+    each(pairs_of[1], "after_twins")
+    win_out(0, 1).start()
+    win_out(1, 1).start()
+    lax.fori_loop(pairs, 2 * pairs, unit, 0)
+    mix(1)
+    w_second(3)
+    for back in range(3):
+        each(queries, "after_over", back)
+    each(queries, "after_twins")
+    for flow in flows:
+        each(flow, "finish")
+    for row in range(2):
+        win_out(2, row).start()
+    for copy in mix_copy:
+        copy.wait()
+    mixed_ref[...] += came[...].astype(f32)
+    w_twin(3).wait_recv()
+    w_pass(3).wait_recv()
+    for m in range(4):
+        w_across(m).wait_send()
+        w_over(m).wait_send()
+        w_twin(m).wait_send()
+        w_pass(m).wait_send()
+    y_tok.wait_send()
+    for row in range(2):
+        for m in range(3):
+            win_out(m, row).wait()
+    w_out_copy.wait()
+    y_cot.wait()
+
+
+def front(tokens, cotangent, doc_ids, small, w_key, w_value, w_query, w_up, w_out, number):
+    dma = pltpu.SemaphoreType.DMA
+    bf16 = jnp.bfloat16
+    chunk, width = tokens.shape
+    half, ff = w_up.shape
+    hbm, vmem = pl.BlockSpec(memory_space=pl.ANY), pl.BlockSpec(memory_space=pltpu.VMEM)
+    window = jax.ShapeDtypeStruct((2, SLOTS * CHUNK, half), bf16)
+    return pl.pallas_call(
+        front_kernel,
+        out_shape=[
+            window,
+            window,
+            window,
+            *[jax.ShapeDtypeStruct((2 * chunk, half), bf16)] * 3,
+            jax.ShapeDtypeStruct((2 * chunk, width), bf16),
+            jax.ShapeDtypeStruct((chunk, width), bf16),
+            jax.ShapeDtypeStruct((chunk, width), bf16),
+            jax.ShapeDtypeStruct(doc_ids.shape, jnp.int32),
+            jax.ShapeDtypeStruct((small.shape[0], width), bf16),
+            jax.ShapeDtypeStruct((3, half, half), bf16),
+            jax.ShapeDtypeStruct((half, ff // 2), bf16),
+            jax.ShapeDtypeStruct((2 * chunk, half), jnp.float32),
+            jax.ShapeDtypeStruct((2 * chunk, half), jnp.float32),
+            jax.ShapeDtypeStruct((2 * chunk, width), jnp.float32),
+            jax.ShapeDtypeStruct((8, 2 * REACH * CHUNK + doc_ids.shape[1]), jnp.int32),
+        ],
+        in_specs=[vmem, hbm, vmem, vmem, hbm, hbm, hbm, hbm, vmem],
+        out_specs=[hbm] * 3 + [vmem] * 5 + [hbm] + [vmem] * 2 + [hbm] * 2 + [vmem] * 4,
+        scratch_shapes=[
+            *[pltpu.VMEM(window.shape, bf16)] * 3,
+            pltpu.VMEM((3, half, half), bf16),
+            pltpu.VMEM((3, half, half), bf16),
+            pltpu.VMEM((2 * chunk, width), bf16),
+            pltpu.VMEM((2 * chunk, width), bf16),
+            pltpu.VMEM((2 * chunk, width), bf16),
+            dma((3,)),
+            dma((2, 4)),
+            dma((2, 4, 4)),
+            dma((6, 2, 12)),
+            dma((2, 2)),
+            dma((4, 2)),
+        ],
+        compiler_params=pltpu.CompilerParams(
+            collective_id=number, has_side_effects=True, vmem_limit_bytes=56 * 2**20
+        ),
+    )(tokens, cotangent, doc_ids, small, w_key, w_value, w_query, w_up, w_out)
+
+
+MESH_ID = pl.DeviceIdType.MESH
+RING = 8
+VEC_ROWS = 16
+CHAINS = (
+    (0, 160, 640, False),
+    (1, 160, 640, False),
+    (0, 80, 1280, True),
+    (1, 80, 1280, True),
+    (0, 80, 640, True),
+    (0, 80, 640, True),
+    (1, 80, 640, True),
+    (1, 80, 640, False),
+)
+EARLY, LATE = (0, 1, 2, 3), (4, 5, 6, 7)
+
+
+def device_at(side, level, column, core):
+    return (side, (level * 2 + column) * 2 + core)
+
+
+def ring_device(side, spot, core):
+    level = jnp.where(spot < 4, spot, 7 - spot)
+    return device_at(side, level, spot // 4, core)
+
+
+def greet(partners):
+    barrier = pltpu.get_barrier_semaphore()
+    for partner in partners:
+        pl.semaphore_signal(barrier, inc=1, device_id=partner, device_id_type=MESH_ID)
+    pl.semaphore_wait(barrier, len(partners))
+
+
+def tile(first, size, step=16):
+    return pl.ds(first if isinstance(first, int) else pl.multiple_of(first, step), size)
+
+
+def remote(source, target, sems, where, device):
+    return pltpu.make_async_remote_copy(
+        source,
+        target,
+        sems.at[(0,) + where],
+        sems.at[(1,) + where],
+        device_id=device,
+        device_id_type=MESH_ID,
+    )
+
+
+class Rings:
+    def __init__(self, side, spot_on_ring, core, devices, source_of, result_of, buffers, sems):
+        self.side, self.spot, self.core = side, spot_on_ring, core
+        self.sibling, self.across, ahead, behind = devices
+        self.targets = (ahead, behind)
+        self.source_of, self.result_of = source_of, result_of
+        self.mine, self.theirs, self.landed, self.swapped = buffers
+        (
+            self.load_sem,
+            self.core_sems,
+            self.ring_sems,
+            self.back_sems,
+            self.share_sems,
+            self.swap_sems,
+            self.keep_sem,
+        ) = sems
+
+    def shard_at(self, chain, offset):
+        return (self.spot + RING + (1 - 2 * CHAINS[chain][0]) * offset) % RING
+
+    def load(self, chain, step):
+        return pltpu.make_async_copy(
+            self.source_of(chain, self.core, self.shard_at(chain, RING - 1 - step)),
+            self.mine[chain].at[step % 3],
+            self.load_sem.at[chain, step % 3],
+        )
+
+    def cross(self, chain, step):
+        return remote(
+            self.source_of(chain, 1 - self.core, self.shard_at(chain, RING - 1 - step)),
+            self.theirs[chain].at[step],
+            self.core_sems,
+            (chain, step),
+            self.sibling,
+        )
+
+    def start_inputs(self, chains, step):
+        for chain in chains:
+            self.load(chain, step).start()
+            self.cross(chain, step).start()
+
+    def ring_copy(self, chain, step):
+        return remote(
+            self.mine[chain].at[step % 3],
+            self.landed[chain].at[step],
+            self.ring_sems,
+            (chain, step),
+            self.targets[CHAINS[chain][0]],
+        )
+
+    def add(self, chain, step, first=False):
+        self.load(chain, step).wait()
+        self.cross(chain, step).wait()
+        f32 = jnp.float32
+        value = self.mine[chain][step % 3].astype(f32) + self.theirs[chain][step].astype(f32)
+        if not first:
+            value = value + self.landed[chain][step - 1].astype(f32)
+        self.mine[chain][step % 3] = value.astype(jnp.bfloat16)
+
+    def begin(self, chains):
+        for chain in chains:
+            self.add(chain, 0, True)
+            self.ring_copy(chain, 0).start()
+        self.start_inputs(chains, 2)
+
+    def middle(self, chains, step):
+        for chain in chains:
+            self.ring_copy(chain, step - 1).wait()
+
+            @pl.when(step < RING - 2)
+            def _():
+                self.load(chain, step + 2).start()
+                self.cross(chain, step + 2).start()
+
+            self.add(chain, step)
+            self.ring_copy(chain, step).start()
+
+    def back_copy(self, chain, step, own=False):
+        shard = self.shard_at(chain, RING - step)
+        return remote(
+            self.mine[chain].at[(RING - 1) % 3] if own else self.result_of(chain, shard),
+            self.result_of(chain, shard),
+            self.back_sems,
+            (chain, step),
+            self.targets[CHAINS[chain][0]],
+        )
+
+    def share(self, chain, step, own=False):
+        shard = self.shard_at(chain, RING - step)
+        return remote(
+            self.mine[chain].at[(RING - 1) % 3] if own else self.result_of(chain, shard),
+            self.result_of(chain, shard),
+            self.share_sems,
+            (chain, step),
+            self.sibling,
+        )
+
+    def keep(self, chain):
+        return pltpu.make_async_copy(
+            self.mine[chain].at[(RING - 1) % 3],
+            self.result_of(chain, self.spot),
+            self.keep_sem.at[chain],
+        )
+
+    def publish(self, chain):
+        self.back_copy(chain, 0, True).start()
+        self.share(chain, 0, True).start()
+        self.keep(chain).start()
+
+    def trade(self, chain):
+        return remote(
+            self.mine[chain].at[(RING - 1) % 3],
+            self.swapped[chain],
+            self.swap_sems,
+            (chain,),
+            self.across,
+        )
+
+    def last(self, chains):
+        for chain in chains:
+            self.ring_copy(chain, RING - 2).wait()
+            self.add(chain, RING - 1)
+            if CHAINS[chain][3]:
+
+                @pl.when(self.core == 1)
+                def _():
+                    self.trade(chain).start()
+
+                @pl.when(self.core == 0)
+                def _():
+                    self.publish(chain)
+
+            else:
+                self.publish(chain)
+
+    def traded(self, chains):
+        for chain in chains:
+            if CHAINS[chain][3]:
+
+                @pl.when(self.core == 1)
+                def _():
+                    self.trade(chain).wait()
+                    self.mine[chain][(RING - 1) % 3] = self.swapped[chain][...]
+                    self.publish(chain)
+
+    def back_begin(self, chains):
+        for chain in chains:
+            self.back_copy(chain, 0, True).wait()
+            self.back_copy(chain, 1).start()
+            self.share(chain, 1).start()
+
+    def back_middle(self, chains, step):
+        for chain in chains:
+            self.back_copy(chain, step).wait()
+
+            @pl.when(step < RING - 2)
+            def _():
+                self.back_copy(chain, step + 1).start()
+
+            self.share(chain, step + 1).start()
+
+    def end(self, chains):
+        for chain in chains:
+            self.keep(chain).wait()
+            self.share(chain, 0, True).wait()
+
+        def rest(step, unused):
+            for chain in chains:
+                self.share(chain, step).wait()
+            return unused
+
+        lax.fori_loop(1, RING, rest, 0)
+
+
+def tail_kernel(
+    gdown_ref,
+    gup_ref,
+    part_two_ref,
+    hidden_ref,
+    small_ref,
+    cot_ref,
+    w_out_ref,
+    attn_ref,
+    lse_ref,
+    q_ref,
+    k_ref,
+    v_ref,
+    kwin_ref,
+    vwin_ref,
+    qwin_ref,
+    ids_ref,
+    ln_ref,
+    wk_ref,
+    wv_ref,
+    wq_ref,
+    w_other_ref,
+    x_ref,
+    bias_up_ref,
+    down_ref,
+    sum_down,
+    sum_out,
+    sum_up,
+    sum_query,
+    sum_key,
+    sum_value,
+    vec_out_ref,
+    grad_input_ref,
+    output_ref,
+    *refs,
+):
+    count = len(CHAINS)
+    buffers = [refs[i * count : (i + 1) * count] for i in range(4)]
+    (
+        dowin,
+        statwin,
+        sent,
+        came,
+        grad_hidden,
+        grad_mix,
+        grad_heads,
+        gout,
+        gqkv,
+        grad_three,
+        w_own,
+        w_other,
+        first_buf,
+        second_buf,
+        grad_one,
+        sums,
+        sent_down,
+        came_down,
+        query_ids,
+        key_ids,
+        later_ids,
+        vec_steps,
+        vec_landed,
+        block_sem,
+        weight_sem,
+        y_sems,
+        do_sems,
+        stat_sems,
+        vec_sems,
+        *ring_sems,
+    ) = refs[4 * count :]
+    f32, bf16 = jnp.float32, jnp.bfloat16
+    side = lax.axis_index("grp")
+    spot = spot_of(lax.axis_index("rep"))
+    level, column, core = spot
+    on_ring = jnp.where(column == 0, level, 7 - level)
+    near_by = neighbours(side, spot)
+    across, sibling, over = near_by[:3]
+    ahead = ring_device(side, (on_ring + 1) % RING, core)
+    behind = ring_device(side, (on_ring + RING - 1) % RING, core)
+    near = device_at(side, level + 1 - 2 * (level % 2), column, core)
+    far = device_at(side, (level + 2) % 4, column, core)
+    vec_partners = (sibling, over, near, far)
+    block = side + core - 2 * side * core
+    half = w_own.shape[1]
+    pairs = half // CHUNK
+    own_cols = tile(half * side, half, 128)
+
+    def source_of(chain, which, shard):
+        if chain < 2:
+            return gdown_ref.at[tile(320 * shard + 160 * chain, 160), tile(640 * which, 640, 128)]
+        rows = tile(640 * which + 80 * shard, 80)
+        if chain < 4:
+            return gup_ref.at[rows, pl.ds(1280 * (chain - 2), 1280)]
+        if chain < 7:
+            return gqkv.at[rows, pl.ds(640 * (chain - 4), 640)]
+        return gout.at[tile(80 * shard, 80), tile(640 * which, 640, 128)]
+
+    def result_of(chain, shard):
+        if chain < 2:
+            return sum_down.at[tile(320 * shard + 160 * chain, 160), tile(640 * core, 640, 128)]
+        rows = tile(80 * shard, 80)
+        if chain < 4:
+            return sum_up.at[rows, tile(2560 * block + 1280 * (chain - 2), 1280, 128)]
+        if chain < 7:
+            return (sum_query, sum_key, sum_value)[chain - 4].at[rows, tile(640 * block, 640, 128)]
+        return sum_out.at[rows, tile(640 * core, 640, 128)]
+
+    rings = Rings(
+        side,
+        on_ring,
+        core,
+        (sibling, across, ahead, behind),
+        source_of,
+        result_of,
+        buffers,
+        ring_sems,
+    )
+    stats = Stream(
+        side, spot, True, lambda slot: statwin.at[:, tile(CHUNK * slot, CHUNK, CHUNK)], stat_sems
+    )
+    grads = Stream(side, spot, True, rows_of(dowin), do_sems)
+    streams = (stats, grads)
+    own_slot = pl.ds((SLOTS - 1) * CHUNK, CHUNK)
+    upper, lower = pl.ds(0, CHUNK), pl.ds(CHUNK, CHUNK)
+
+    def exchange(which):
+        return (
+            remote(sent.at[lower], came.at[which, upper], y_sems, (which, 0), across),
+            remote(sent.at[upper], came.at[which, lower], y_sems, (which, 1), across),
+        )
+
+    down_copy = remote(sent_down, came_down, y_sems, (2, 0), across)
+    dowin[...] = jnp.zeros_like(dowin)
+    statwin[...] = jnp.zeros_like(statwin)
+    sent[...] = part_two_ref[...].astype(bf16)
+    greet(near_by + far_corners(side, spot) + (far, ahead, behind))
+    for copy in exchange(0):
+        copy.start()
+    sent_down[...] = down_ref[CHUNK:, :].astype(bf16)
+    down_copy.start()
+    rings.start_inputs(EARLY, 0)
+    rings.start_inputs(EARLY, 1)
+    weights = (wq_ref, wk_ref, wv_ref)
+    weight_loads = [
+        pltpu.make_async_copy(weights[m].at[:, own_cols], w_own.at[m], weight_sem.at[m])
+        for m in range(3)
+    ] + [
+        pltpu.make_async_copy(w_other_ref.at[(m + 2) % 3], w_other.at[m], weight_sem.at[3 + m])
+        for m in range(3)
+    ]
+    for copy in weight_loads:
+        copy.start()
+    rings.begin(EARLY)
+
+    for row in range(2):
+        line = slice(row, row + 1)
+        first = REACH * CHUNK
+        own = ids_ref[line, tile(first + CHUNK * lax.axis_index("rep"), CHUNK, CHUNK)].astype(f32)
+        query_ids[row] = jnp.broadcast_to(own, (CHUNK, CHUNK)).T
+        key_ids[row] = ids_ref[line, tile(CHUNK * lax.axis_index("rep"), WINDOW, CHUNK)].astype(f32)
+        for k in range(REACH + 1):
+            at = tile(first + CHUNK * (lax.axis_index("rep") + k), CHUNK, CHUNK)
+            later_ids[row, :, (REACH - k) * CHUNK : (REACH + 1 - k) * CHUNK] = ids_ref[
+                line, at
+            ].astype(f32)
+
+    def back_through_norm(which, part_ref, input_ref, gain_line, base, finish):
+        zero = jnp.zeros((8, part_ref.shape[1]), f32)
+
+        def some_rows(i, carry):
+            rows = tile(32 * i, 32, 32)
+            grad = part_ref[rows, :] + came[which, rows, :].astype(f32)
+            inputs = input_ref[rows, :].astype(f32)
+            center = inputs - jnp.mean(inputs, axis=-1, keepdims=True)
+            inverse = lax.rsqrt(jnp.mean(center * center, axis=-1, keepdims=True) + EPSILON)
+            normed = center * inverse
+            scaled = grad * small_ref[gain_line : gain_line + 1, :].astype(f32)
+            value = inverse * (
+                scaled
+                - jnp.mean(scaled, axis=-1, keepdims=True)
+                - normed * jnp.mean(scaled * normed, axis=-1, keepdims=True)
+            )
+            extra = finish(rows, value)
+            parts = [grad * normed, grad] + extra
+            return tuple(
+                c + jnp.sum(p.reshape(4, 8, -1), axis=0) for c, p in zip(carry, parts)
+            )
+
+        totals = lax.fori_loop(0, 8, some_rows, (zero,) * (3 if base == 0 else 2))
+        for k, total in enumerate(totals):
+            sums[base + k : base + k + 1, :] = jnp.sum(total, axis=0, keepdims=True)
+
+    def finish_two(rows, value):
+        hidden = cot_ref[rows, :].astype(f32) + value
+        low = hidden.astype(bf16)
+        grad_hidden[rows, :] = hidden
+        grad_mix[rows, :] = low
+        return [low.astype(f32)]
+
+    rings.middle(EARLY, 1)
+    for copy in exchange(0):
+        copy.wait()
+    back_through_norm(0, part_two_ref, hidden_ref, 4, 0, finish_two)
+    grad_heads[...] = matmul_nt(grad_mix[...], w_out_ref[...]).astype(bf16)
+
+    def own_stats(i, unused):
+        row, pair = i // pairs, i % pairs
+        rows, lanes = tile(CHUNK * row, CHUNK, CHUNK), tile(CHUNK * pair, CHUNK, CHUNK)
+        weighed = (grad_heads[rows, lanes].astype(f32) * attn_ref[rows, lanes]).T
+        level_of = lse_ref[rows, lanes].T
+        zero = jnp.zeros((4, CHUNK), f32)
+        statwin[tile(8 * i, 8, 8), own_slot] = jnp.concatenate(
+            [
+                level_of[:1],
+                level_of[HALF_LANES : HALF_LANES + 1],
+                jnp.sum(weighed[:HALF_LANES], axis=0, keepdims=True),
+                jnp.sum(weighed[HALF_LANES:], axis=0, keepdims=True),
+                zero,
+            ],
+            axis=0,
+        )
+        return unused
+
+    lax.fori_loop(0, 2 * pairs, own_stats, 0)
+    dowin[0, own_slot, :] = grad_heads[:CHUNK, :]
+    dowin[1, own_slot, :] = grad_heads[CHUNK:, :]
+    for stream in streams:
+        stream.start_own()
+
+    window = pl.ds((SLOTS - 1 - REACH) * CHUNK, WINDOW)
+
+    def block_loads(refs_bufs, i):
+        row, pair = i // pairs, i % pairs
+        lanes = tile(CHUNK * pair, CHUNK, CHUNK)
+        return [
+            pltpu.make_async_copy(
+                ref.at[row, window, lanes], buf.at[i % 2], block_sem.at[k, i % 2]
+            )
+            for k, (ref, buf) in enumerate(refs_bufs)
+        ]
+
+    kv_blocks = ((kwin_ref, first_buf), (vwin_ref, second_buf))
+    q_blocks = ((qwin_ref, first_buf),)
+
+    def start_blocks(refs_bufs, i):
+        for copy in block_loads(refs_bufs, i):
+            copy.start()
+
+    def use_blocks(refs_bufs, i):
+        for copy in block_loads(refs_bufs, i):
+            copy.wait()
+        pl.when(i + 1 < 2 * pairs)(lambda: start_blocks(refs_bufs, i + 1))
+
+    scale = HEAD_DIM**-0.5
+    start_blocks(kv_blocks, 0)
+    attn_low = attn_ref[...].astype(bf16)
+    gout[...] = matmul_tn(attn_low, grad_mix[...]).astype(bf16)
+
+    def query_unit(i, unused):
+        row, pair = i // pairs, i % pairs
+        rows, lanes = tile(CHUNK * row, CHUNK, CHUNK), tile(CHUNK * pair, CHUNK, CHUNK)
+        use_blocks(kv_blocks, i)
+        query = q_ref[rows, lanes] * jnp.bfloat16(scale)
+        keys, values = first_buf[i % 2], second_buf[i % 2]
+        grad = grad_heads[rows, lanes]
+        allowed = (query_ids[row][:, :1] == key_ids[row]) & (
+            iota((CHUNK, WINDOW), 1) <= iota((CHUNK, WINDOW), 0) + REACH * CHUNK
+        )
+        weighed = grad.astype(f32) * attn_ref[rows, lanes]
+        lse_pair = lse_ref[rows, lanes]
+        parts = []
+        for which in range(2):
+            lse = lse_pair[:, which * HALF_LANES : which * HALF_LANES + 1]
+            delta = jnp.sum(head_half(weighed, which), axis=-1, keepdims=True)
+            scores = jnp.where(allowed, matmul_nt(head_half(query, which), keys), NEGATIVE)
+            probs = jnp.exp(scores - lse)
+            grad_probs = matmul_nt(head_half(grad, which), values)
+            grad_scores = (probs * (grad_probs - delta)).astype(bf16)
+            parts.append(matmul(grad_scores, keys))
+        grad_three[0, rows, lanes] = (join_halves(*parts) * scale).astype(bf16)
+        events = {
+            1: (lambda s: s.after_up(0),),
+            5: (lambda s: s.after_over(0), lambda s: s.after_up(1)),
+            9: (lambda s: s.after_over(1),),
+        }
+        for at, what in events.items():
+
+            @pl.when(i == at)
+            def _():
+                rings.middle(EARLY, 2 + at // 4)
+                for event in what:
+                    for stream in streams:
+                        event(stream)
+
+        return unused
+
+    lax.fori_loop(0, 2 * pairs, query_unit, 0)
+    start_blocks(q_blocks, 0)
+    rings.middle(EARLY, 5)
+    for stream in streams:
+        stream.after_over(2)
+    for stream in streams:
+        stream.after_twins()
+
+    def key_unit(i, unused):
+        row, pair = i // pairs, i % pairs
+        rows, lanes = tile(CHUNK * row, CHUNK, CHUNK), tile(CHUNK * pair, CHUNK, CHUNK)
+        use_blocks(q_blocks, i)
+        keys = k_ref[rows, lanes] * jnp.bfloat16(scale)
+        values = v_ref[rows, lanes]
+        queries = first_buf[i % 2]
+        after = dowin[row, window, lanes]
+        lane = iota((CHUNK, WINDOW), 1)
+        ahead_by = (REACH - lane // CHUNK) * CHUNK + lane % CHUNK
+        allowed = (query_ids[row][:, :1] == later_ids[row]) & (ahead_by >= iota((CHUNK, WINDOW), 0))
+        lines = statwin[tile(8 * i, 8, 8), window]
+        key_parts, value_parts = [], []
+        for which in range(2):
+            lse, delta = lines[which : which + 1], lines[2 + which : 3 + which]
+            scores = jnp.where(allowed, matmul_nt(head_half(keys, which), queries), NEGATIVE)
+            probs = jnp.exp(scores - lse)
+            value_parts.append(matmul(probs.astype(bf16), after))
+            grad_probs = matmul_nt(head_half(values, which), after)
+            grad_scores = (probs * (grad_probs - delta)).astype(bf16)
+            key_parts.append(matmul(grad_scores, queries))
+        grad_three[1, rows, lanes] = (join_halves(*key_parts) * scale).astype(bf16)
+        grad_three[2, rows, lanes] = join_halves(*value_parts).astype(bf16)
+        pl.when(i == 3)(lambda: rings.middle(EARLY, 6))
+        pl.when(i == 8)(lambda: rings.last(EARLY))
+        return unused
+
+    lax.fori_loop(0, 2 * pairs, key_unit, 0)
+    rings.traded(EARLY)
+    for stream in streams:
+        stream.finish()
+
+    for copy in weight_loads:
+        copy.wait()
+    rings.back_begin(EARLY)
+    for m in range(3):
+
+        def weight_rows(i, unused):
+            lanes = tile(256 * i, 256, 256)
+            gqkv[lanes, m * half : (m + 1) * half] = matmul_tn(
+                ln_ref[:, lanes], grad_three[m]
+            ).astype(bf16)
+            return unused
+
+        lax.fori_loop(0, 2 * half // 256, weight_rows, 0)
+    rings.start_inputs(LATE, 0)
+    rings.start_inputs(LATE, 1)
+    rings.begin(LATE)
+
+    own_part, other_part = 0.0, 0.0
+    for m in range(3):
+        own_part = own_part + matmul_nt(grad_three[m], w_own[m])
+        other_part = other_part + matmul_nt(grad_three[m], w_other[m])
+    grad_one[:, own_cols] = own_part
+    grad_one[:, tile(half * (1 - side), half, 128)] = other_part
+    sent[...] = grad_one[...].astype(bf16)
+    for copy in exchange(1):
+        copy.start()
+    for k, m in ((0, 0), (1, 2)):
+        sums[6 + k : 7 + k, :half] = jnp.sum(grad_three[m].astype(f32), axis=0, keepdims=True)
+
+    def both_rings(step, unused):
+        rings.back_middle(EARLY, step)
+        rings.middle(LATE, step)
+        return unused
+
+    both_rings(jnp.int32(1), 0)
+    for copy in exchange(1):
+        copy.wait()
+
+    def finish_one(rows, value):
+        grad_hidden[rows, :] = grad_hidden[rows, :] + value
+        return []
+
+    back_through_norm(1, grad_one, x_ref, 2, 3, finish_one)
+    grad_input_ref[...] = grad_hidden[:CHUNK, :]
+    sums[5:6, :] = jnp.sum(cot_ref[...].astype(f32), axis=0, keepdims=True)
+    vec_steps[0] = jnp.zeros(vec_steps.shape[1:], f32)
+    for k in range(4):
+        vec_steps[0, 3 + k : 4 + k, :] = bias_up_ref[:1, k * half : (k + 1) * half]
+    for row, (line, cols) in {
+        0: (6, pl.ds(0, half)),
+        1: (7, pl.ds(0, half)),
+        2: (2, own_cols),
+        7: (5, own_cols),
+        8: (3, own_cols),
+        9: (4, own_cols),
+        10: (0, own_cols),
+        11: (1, own_cols),
+    }.items():
+        vec_steps[0, row : row + 1, :] = sums[line : line + 1, cols]
+    vec_copy = [
+        remote(vec_steps.at[k], vec_landed.at[k], vec_sems, (k,), vec_partners[k])
+        for k in range(4)
+    ]
+    vec_copy[0].start()
+    for k in range(4):
+        both_rings(jnp.int32(2 + k), 0)
+        vec_copy[k].wait()
+        vec_steps[k + 1] = vec_steps[k] + vec_landed[k]
+        if k < 3:
+            vec_copy[k + 1].start()
+    vec_out_ref[...] = vec_steps[4]
+    both_rings(jnp.int32(6), 0)
+    rings.last(LATE)
+    rings.end(EARLY)
+    down_copy.wait()
+    output_ref[...] = (
+        hidden_ref[:CHUNK, :]
+        + down_ref[:CHUNK, :]
+        + came_down[...].astype(f32)
+        + small_ref[1:2, :].astype(f32)
+    ).astype(bf16)
+    rings.traded(LATE)
+    rings.back_begin(LATE)
+
+    def late_back(step, unused):
+        rings.back_middle(LATE, step)
+        return unused
+
+    lax.fori_loop(1, RING - 1, late_back, 0)
+    rings.end(LATE)
+
+
+def tail(operands, width, half, ff, number):
+    dma = pltpu.SemaphoreType.DMA
+    f32, bf16 = jnp.float32, jnp.bfloat16
+    count = len(CHAINS)
+    rows = operands[3].shape[0]
+    hbm, vmem = pl.BlockSpec(memory_space=pl.ANY), pl.BlockSpec(memory_space=pltpu.VMEM)
+    in_hbm = (0, 1, 12, 13, 14, 17, 18, 19, 20)
+    square = jax.ShapeDtypeStruct((half, width), bf16)
+
+    def room(depth):
+        return [pltpu.VMEM(depth + (tall, wide), bf16) for _, tall, wide, _ in CHAINS]
+
+    return pl.pallas_call(
+        tail_kernel,
+        out_shape=[
+            jax.ShapeDtypeStruct((ff, width), bf16),
+            square,
+            jax.ShapeDtypeStruct((half, 2 * ff), bf16),
+            square,
+            square,
+            square,
+            jax.ShapeDtypeStruct((VEC_ROWS, half), f32),
+            jax.ShapeDtypeStruct((CHUNK, width), f32),
+            jax.ShapeDtypeStruct((CHUNK, width), bf16),
+        ],
+        in_specs=[hbm if i in in_hbm else vmem for i in range(len(operands))],
+        out_specs=[hbm] * 6 + [vmem] * 3,
+        scratch_shapes=[
+            *room((3,)),
+            *room((RING,)),
+            *room((RING - 1,)),
+            *room(()),
+            pltpu.VMEM((2, SLOTS * CHUNK, half), bf16),
+            pltpu.VMEM((16 * half // CHUNK, SLOTS * CHUNK), f32),
+            pltpu.VMEM((rows, width), bf16),
+            pltpu.VMEM((2, rows, width), bf16),
+            pltpu.VMEM((rows, width), f32),
+            pltpu.VMEM((rows, width), bf16),
+            pltpu.VMEM((rows, half), bf16),
+            pltpu.VMEM((half, width), bf16),
+            pltpu.VMEM((width, 3 * half), bf16),
+            pltpu.VMEM((3, rows, half), bf16),
+            pltpu.VMEM((3, half, half), bf16),
+            pltpu.VMEM((3, half, half), bf16),
+            pltpu.VMEM((2, WINDOW, CHUNK), bf16),
+            pltpu.VMEM((2, WINDOW, CHUNK), bf16),
+            pltpu.VMEM((rows, width), f32),
+            pltpu.VMEM((8, width), f32),
+            pltpu.VMEM((CHUNK, width), bf16),
+            pltpu.VMEM((CHUNK, width), bf16),
+            pltpu.VMEM((2, CHUNK, CHUNK), f32),
+            pltpu.VMEM((2, 1, WINDOW), f32),
+            pltpu.VMEM((2, 1, WINDOW), f32),
+            pltpu.VMEM((5, VEC_ROWS, half), f32),
+            pltpu.VMEM((4, VEC_ROWS, half), f32),
+            dma((2, 2)),
+            dma((6,)),
+            dma((2, 3, 2)),
+            dma((2, 12)),
+            dma((2, 12)),
+            dma((2, 4)),
+            dma((count, 3)),
+            dma((2, count, RING)),
+            dma((2, count, RING - 1)),
+            dma((2, count, RING - 1)),
+            dma((2, count, RING)),
+            dma((2, count)),
+            dma((count,)),
+        ],
+        compiler_params=pltpu.CompilerParams(
+            collective_id=number, has_side_effects=True, vmem_limit_bytes=60 * 2**20
+        ),
+    )(*operands)
+
+
+FF_BLOCK = 512
+
+
+def ff_kernel(
+    side_ref,
+    tok_ref,
+    tok_other_ref,
+    mixed_ref,
+    small_ref,
+    cot_ref,
+    cot_other_ref,
+    up_own_ref,
+    up_other_ref,
+    down_ref,
+    bias_ref,
+    hidden_ref,
+    x_ref,
+    cot_all_ref,
+    result_ref,
+    back_ref,
+    grad_up_ref,
+    grad_down_ref,
+    grad_bias_ref,
+    ln_ref,
+    own_first,
+    turned,
+):
+    f32, bf16 = jnp.float32, jnp.bfloat16
+    side = side_ref[0]
+    step = pl.program_id(0)
+    chunk, width = tok_ref.shape
+    half = width // 2
+    own_cols, other_cols = tile(half * side, half, 128), tile(half * (1 - side), half, 128)
+
+    @pl.when(step == 0)
+    def _():
+        x_ref[:chunk, :] = tok_ref[...]
+        x_ref[chunk:, :] = tok_other_ref[...]
+        cot_all_ref[:chunk, :] = cot_ref[...]
+        cot_all_ref[chunk:, :] = cot_other_ref[...]
+
+        def some_rows(i, unused):
+            rows = tile(32 * i, 32, 32)
+            hidden = x_ref[rows, :].astype(f32) + mixed_ref[rows, :] + small_ref[:1, :].astype(f32)
+            hidden_ref[rows, :] = hidden
+            normed, _ = norm_rows(hidden)
+            ln_ref[rows, :] = (
+                normed * small_ref[4:5, :].astype(f32) + small_ref[5:6, :].astype(f32)
+            ).astype(bf16)
+            return unused
+
+        lax.fori_loop(0, 2 * chunk // 32, some_rows, 0)
+        own_first[:, :half] = ln_ref[:, own_cols]
+        own_first[:, half:] = ln_ref[:, other_cols]
+        turned[...] = own_first[...].T
+        result_ref[...] = jnp.zeros_like(result_ref)
+        back_ref[...] = jnp.zeros_like(back_ref)
+
+    pre_act = (
+        matmul(own_first[:, :half], up_own_ref[...])
+        + matmul(own_first[:, half:], up_other_ref[...])
+        + bias_ref[...].astype(f32)
+    )
+    value, slope = gelu_pair(pre_act)
+    act = value.astype(bf16)
+    cot = cot_all_ref[...]
+    result_ref[...] += matmul(act, down_ref[...])
+    grad_pre = (matmul_nt(cot, down_ref[...]) * slope).astype(bf16)
+    grad_bias_ref[...] = jnp.sum(grad_pre.astype(f32), axis=0, keepdims=True)
+    grad_down_ref[...] = matmul_tn(act, cot).astype(bf16)
+    grad_up_ref[...] = matmul(turned[...], grad_pre).astype(bf16)
+    back_ref[:, own_cols] += matmul_nt(grad_pre, up_own_ref[...])
+    back_ref[:, other_cols] += matmul_nt(grad_pre, up_other_ref[...])
+
+
+def feed_forward(side, tokens, tok_other, mixed, small, cotangent, cot_other, w_up, up_other, w_down, b_up):
+    f32, bf16 = jnp.float32, jnp.bfloat16
+    chunk, width = tokens.shape
+    half = width // 2
+    ff = w_down.shape[0]
+    steps = ff // FF_BLOCK
+
+    def whole(shape):
+        return pl.BlockSpec(shape, lambda j, s: (0, 0))
+
+    rows = 2 * chunk
+    columns = pl.BlockSpec((half, FF_BLOCK), lambda j, s: (0, j))
+    return pl.pallas_call(
+        ff_kernel,
+        grid_spec=pltpu.PrefetchScalarGridSpec(
+            num_scalar_prefetch=1,
+            grid=(steps,),
+            in_specs=[
+                whole((chunk, width)),
+                whole((chunk, width)),
+                whole((rows, width)),
+                whole(small.shape),
+                whole((chunk, width)),
+                whole((chunk, width)),
+                pl.BlockSpec((half, FF_BLOCK), lambda j, s: (0, s[0] * steps + j)),
+                columns,
+                pl.BlockSpec((FF_BLOCK, width), lambda j, s: (j, 0)),
+                pl.BlockSpec((1, FF_BLOCK), lambda j, s: (0, j)),
+            ],
+            out_specs=[
+                whole((rows, width)),
+                whole((rows, width)),
+                whole((rows, width)),
+                whole((rows, width)),
+                whole((rows, width)),
+                pl.BlockSpec((width, FF_BLOCK), lambda j, s: (0, j)),
+                pl.BlockSpec((FF_BLOCK, width), lambda j, s: (j, 0)),
+                pl.BlockSpec((1, FF_BLOCK), lambda j, s: (0, j)),
+            ],
+            scratch_shapes=[
+                pltpu.VMEM((rows, width), bf16),
+                pltpu.VMEM((rows, width), bf16),
+                pltpu.VMEM((width, rows), bf16),
+            ],
+        ),
+        out_shape=[
+            jax.ShapeDtypeStruct((rows, width), f32),
+            jax.ShapeDtypeStruct((rows, width), bf16),
+            jax.ShapeDtypeStruct((rows, width), bf16),
+            jax.ShapeDtypeStruct((rows, width), f32),
+            jax.ShapeDtypeStruct((rows, width), f32),
+            jax.ShapeDtypeStruct((width, ff), bf16),
+            jax.ShapeDtypeStruct((ff, width), bf16),
+            jax.ShapeDtypeStruct((1, ff), f32),
+        ],
+        compiler_params=pltpu.CompilerParams(vmem_limit_bytes=56 * 2**20),
+    )(
+        side.reshape(1).astype(jnp.int32),
+        tokens,
+        tok_other,
+        mixed,
+        small,
+        cotangent,
+        cot_other,
+        w_up,
+        up_other,
+        w_down,
+        b_up.reshape(1, -1),
+    )
+
+
+def widen_kernel(*refs):
+    count = len(refs) // 2
+    for source, target in zip(refs[:count], refs[count:]):
+        target[...] = source[...].astype(jnp.float32)
+
+
+def widen(arrays):
+    steps = 4
+    specs = [
+        pl.BlockSpec((a.shape[0] // steps, a.shape[1]), lambda j: (j, 0)) for a in arrays
+    ]
+    return pl.pallas_call(
+        widen_kernel,
+        grid=(steps,),
+        in_specs=specs,
+        out_specs=specs,
+        out_shape=[jax.ShapeDtypeStruct(a.shape, jnp.float32) for a in arrays],
+        compiler_params=pltpu.CompilerParams(vmem_limit_bytes=56 * 2**20),
+    )(*arrays)
+
+
+def pair_shards(
+    tokens,
+    doc_ids,
+    w_query,
+    w_key,
+    w_value,
+    w_out,
+    w_up,
+    w_down,
+    b_query,
+    b_value,
+    b_out,
+    b_up,
+    b_down,
+    attn_gain,
+    attn_beta,
+    ffn_gain,
+    ffn_beta,
+    cotangent,
+):
+    f32, bf16 = jnp.float32, jnp.bfloat16
+    chunk, width = tokens.shape
+    half = width // 2
+    side = lax.axis_index("grp")
+    row_of_small = lax.broadcasted_iota(jnp.int32, (16, half), 0)
+    small = jnp.zeros((16, half), bf16)
+    for line, vector in enumerate(
+        (b_out, b_down, attn_gain, attn_beta, ffn_gain, ffn_beta, b_query, b_value)
+    ):
+        small = jnp.where(row_of_small == line, vector[None, :], small)
+    (
+        k_win,
+        v_win,
+        q_win,
+        k_own,
+        v_own,
+        q_own,
+        ln_one,
+        tok_other,
+        cot_other,
+        ids_other,
+        small,
+        w_other,
+        w_up_other,
+        attn,
+        lse,
+        mixed,
+        ids,
+    ) = front(tokens, cotangent, doc_ids, small, w_key, w_value, w_query, w_up, w_out, 2)
+    hidden, x_all, cot_all, down, back_two, grad_w_up, grad_w_down, grad_b_up = feed_forward(
+        side, tokens, tok_other, mixed, small, cotangent, cot_other, w_up, w_up_other, w_down, b_up
+    )
+    *sums, vec_sum, grad_input, output = tail(
+        (
+            grad_w_down,
+            grad_w_up,
+            back_two,
+            hidden,
+            small,
+            cot_all,
+            w_out,
+            attn,
+            lse,
+            q_own,
+            k_own,
+            v_own,
+            k_win,
+            v_win,
+            q_win,
+            ids,
+            ln_one,
+            w_key,
+            w_value,
+            w_query,
+            w_other,
+            x_all,
+            grad_b_up,
+            down,
+        ),
+        width,
+        half,
+        w_down.shape[0],
+        1,
+    )
+    sum_down, sum_out, sum_up, sum_query, sum_key, sum_value = widen(sums)
+    cuts = [
+        vec_sum[at : at + size].reshape(-1)
+        for at, size in ((0, 1), (1, 1), (2, 1), (3, 4), (7, 1), (8, 1), (9, 1), (10, 1), (11, 1))
+    ]
+    return (
+        output,
+        grad_input,
+        sum_query,
+        sum_key,
+        sum_value,
+        sum_out,
+        sum_up,
+        sum_down,
+        *cuts,
+    )
+
+
 def solution(mesh):
     in_specs = (
         P(("grp", "rep"), None),
@@ -473,4 +1980,5 @@
         P("grp"),
         P("grp"),
     )
-    return jax.shard_map(shards, mesh=mesh, in_specs=in_specs, out_specs=out_specs, check_vma=False)
+    plan = pair_shards if fits_pair(mesh) else shards
+    return jax.shard_map(plan, mesh=mesh, in_specs=in_specs, out_specs=out_specs, check_vma=False)

time: 1690 us -> 376 us (0.22)
  waiting for transfers between devices: 1200 us -> 0 us
  Pallas kernels: 0 us -> 370 us
  matrix products: 134 us -> 0 us
  blocking collectives: 112 us -> 0 us
  starting transfers between devices: 96.5 us -> 0 us
  local copies, waits for them, and re-layouts: 65.3 us -> 3.45 us
  other arithmetic: 50.3 us -> 1.52 us
    reduce_scatter x6 -> x0, waiting for transfers between devices: 415 us -> none  [the longest x1 153 us: shards(): lax.psum_scatter(grad_w_up.astype(jnp.bfloat16), 'grp', scatter_dimension...]
    pallas_call x0 -> x4, Pallas kernels: none -> 370 us  [the longest x1 242 us: tail(): pl.pallas_call(tail_kernel, out_shape=[jax.ShapeDtypeStruct((ff, width),...]
    ppermute x30 -> x0, waiting for transfers between devices: 275 us -> none  [the longest x18 161 us: from_behind(): return lax.ppermute(array, axis, pairs)]
    all_gather x6 -> x0, waiting for transfers between devices: 259 us -> none  [the longest x1 151 us: shards(): lax.all_gather(w_down, 'grp', axis=0, tiled=True)]
    psum x1 -> x0, waiting for transfers between devices: 248 us -> none  [shards(): lax.psum(shares[0].astype(jnp.bfloat16), 'rep').astype(jnp.float32)]
    dot_general x53 -> x0, matrix products: 134 us -> none  [the longest x6 30 us: matmul_nt(): lax.dot_general(left, right, (((1,), (1,)), ((), ())), preferred_element_...]
    ppermute x30 -> x0, starting transfers between devices: 96 us -> none  [the longest x18 78.7 us: from_behind(): return lax.ppermute(array, axis, pairs)]
    psum x1 -> x0, blocking collectives: 62.9 us -> none  [shards(): lax.psum(shares[6].astype(jnp.bfloat16), 'rep').astype(jnp.float32)]
  transfers between devices with their start and end apart: 43 -> 0, of which waited for: 39 -> 0; matrix products, arithmetic and copies ran while one was open for 10% -> 0% of each run, Pallas kernels for 0% -> 0%
where the time goes in v3:
time: 376 us
  Pallas kernels  370 us (98%)
    pallas_call x1, Pallas kernels, tail(): pl.pallas_call(tail_kernel, out_shape=[jax.ShapeDtypeStruct((ff, width),...  242 us
    pallas_call x1, Pallas kernels, front(): pl.pallas_call(front_kernel, out_shape=[window, window, window, *[jax.Sha...  88.4 us
    pallas_call x1, Pallas kernels, feed_forward(): pl.pallas_call(ff_kernel, grid_spec=pltpu.PrefetchScalarGridSpec(num_scal...  21 us
    pallas_call x1, Pallas kernels, widen(): pl.pallas_call(widen_kernel, grid=(steps,), in_specs=specs, out_specs=spe...  18.7 us

profile of v3, /device:TPU:0, one launch (start us, length us, event | category | flops | bytes accessed | tf_op | source)
XLA Modules:
  0.0 375.7 jit_solution(1501922538466524404)
XLA Ops:
  0.7 1.5 select_select_fusion.small_ref
  2.2 0.0 copy-start.3
  2.2 88.4 %shard_map.305 = (bf16[2,1536,640]{2,1,0:T(8,128)(2,1)}, bf16[2,1536,640]{2,1,0:T(8,128)(2,1)}, bf16[2,1536,640]{2,1,0:T(8,128)(2,1)}, bf16[256,640]{1,0:T(8,128...) custom-call(bf16[128,1280]{1,0:T(8,128)(2,1)} %tok_ref.3, ...), custom_call_target="tpu_custom_call" | custom-call | tf_op jit(solution)/shard_map/pallas_call | solution.py:909
  90.7 0.0 copy-done.3
  90.7 0.6 reshape.76.bias_ref
  91.3 21.0 %shard_map.306 = (f32[256,1280]{1,0:T(8,128)}, bf16[256,1280]{1,0:T(8,128)(2,1)}, bf16[256,1280]{1,0:T(8,128)(2,1)}, f32[256,1280]{1,0:T(8,128)}, f32[256,1280]{...) custom-call(s32[1]{0:T(128)} %bitcast.side_ref, ...), custom_call_target="tpu_custom_call" | custom-call | tf_op jit(solution)/shard_map/pallas_call | solution.py:1761
  112.3 241.8 %shard_map.307 = (bf16[2560,1280]{1,0:T(8,128)(2,1)}, bf16[640,1280]{1,0:T(8,128)(2,1)}, bf16[640,5120]{1,0:T(8,128)(2,1)}, bf16[640,1280]{1,0:T(8,128)(2,1)}, b...) custom-call(bf16[2560,1280]{1,0:T(8,128)(2,1)} %get-tuple-element.61, ...), custom_call_target="tpu_custom_call" | custom-call | tf_op jit(solution)/shard_map/pallas_call | solution.py:1611
  354.1 0.0 copy-start.2
  354.1 0.0 copy-start.1
  354.2 0.0 copy-start
  354.2 18.7 %shard_map.308 = (f32[2560,1280]{1,0:T(8,128)}, f32[640,1280]{1,0:T(8,128)}, f32[640,5120]{1,0:T(8,128)}, f32[640,1280]{1,0:T(8,128)}, f32[640,1280]{1,0:T(8,128)}, /*index=5*/f32[640,1280]{1,0:T(8,128)}) custom-call(bf16[2560,1280]{1,0:T(8,128)(2,1)} %get-tuple-element.82.refs_0_, bf16[640,1280]{1,0:T(8,128)(2,1)} %get-tuple-element.83.refs_1_, ...), custom_call_target="tpu_custom_call" | custom-call | tf_op jit(solution)/shard_map/pallas_call | solution.py:1831
  372.8 0.0 copy-done.2
  372.8 0.7 slice_reduce_fusion
  373.5 0.6 reshape.80
  374.1 0.0 copy-done.1
  374.1 0.7 copy.37
  374.8 0.0 copy-done
  374.8 0.8 copy.38
  (5 shorter events, 0.0 us)
Async XLA Ops:
  2.2 88.5 %copy-start.3 = (bf16[2560]{0:T(1024)(128)(2,1)S(1)}, bf16[2560]{0:T(1024)(128)(2,1)}, u32[]{:S(2)}) copy-start(bf16[2560]{0:T(1024)(128)(2,1)} %param.29) | copy-start | bytes 15364
  354.1 18.7 %copy-start.2 = (f32[16,640]{1,0:T(8,128)S(1)}, f32[16,640]{1,0:T(8,128)}, u32[]{:S(2)}) copy-start(f32[16,640]{1,0:T(8,128)} %get-tuple-element.94) | copy-start | bytes 122884
  354.1 20.0 %copy-start.1 = (bf16[128,1280]{1,0:T(8,128)(2,1)S(1)}, bf16[128,1280]{1,0:T(8,128)(2,1)}, u32[]{:S(2)}) copy-start(bf16[128,1280]{1,0:T(8,128)(2,1)} %get-tuple-element.128) | copy-start | bytes 983044
  354.2 20.7 %copy-start = (f32[128,1280]{1,0:T(8,128)S(1)}, f32[128,1280]{1,0:T(8,128)}, u32[]{:S(2)}) copy-start(f32[128,1280]{1,0:T(8,128)} %get-tuple-element.129) | copy-start | bytes 1966084

commit v4 on v3

--- a/solution.py
+++ b/solution.py
@@ -795,9 +795,9 @@
     w_forward(2)
     w_across(3).start()
     y_cot.start()
+    each(pairs_of[1], "after_up", 0)
     each(pairs_of[0], "after_over", 0)
     w_second(2)
-    each(pairs_of[1], "after_up", 0)
     w_ready(2)
     project(2, 0)
     project(2, 1)
@@ -810,9 +810,9 @@
     each(pairs_of[0], "after_over", 1)
     each(queries, "after_up", 0, light)
     w_forward(3)
+    each(queries, "after_up", 1, light)
     each(pairs_of[0], "after_over", 2)
     each(pairs_of[1], "after_over", 1)
-    each(queries, "after_up", 1, light)
     for back in range(3):
         each(queries, "start_over", back, jnp.logical_not(light))
     y_ids.wait()
@@ -873,9 +873,9 @@
     win_out(1, 1).start()
     lax.fori_loop(pairs, 2 * pairs, unit, 0)
     mix(1)
-    w_second(3)
     for back in range(3):
         each(queries, "after_over", back)
+    w_second(3)
     each(queries, "after_twins")
     for flow in flows:
         each(flow, "finish")
@@ -1304,11 +1304,9 @@
     statwin[...] = jnp.zeros_like(statwin)
     sent[...] = part_two_ref[...].astype(bf16)
     greet(near_by + far_corners(side, spot) + (far, ahead, behind))
+    rings.start_inputs(EARLY, 0)
     for copy in exchange(0):
         copy.start()
-    sent_down[...] = down_ref[CHUNK:, :].astype(bf16)
-    down_copy.start()
-    rings.start_inputs(EARLY, 0)
     rings.start_inputs(EARLY, 1)
     weights = (wq_ref, wk_ref, wv_ref)
     weight_loads = [
@@ -1321,6 +1319,8 @@
     for copy in weight_loads:
         copy.start()
     rings.begin(EARLY)
+    sent_down[...] = down_ref[CHUNK:, :].astype(bf16)
+    down_copy.start()
 
     for row in range(2):
         line = slice(row, row + 1)

time: 376 us -> 373 us (level)
  no operation moved by 1% of the time
where the time goes in v4:
time: 373 us
  Pallas kernels  367 us (98%)
    pallas_call x1, Pallas kernels, tail(): pl.pallas_call(tail_kernel, out_shape=[jax.ShapeDtypeStruct((ff, width),...  240 us
    pallas_call x1, Pallas kernels, front(): pl.pallas_call(front_kernel, out_shape=[window, window, window, *[jax.Sha...  87.5 us
    pallas_call x1, Pallas kernels, feed_forward(): pl.pallas_call(ff_kernel, grid_spec=pltpu.PrefetchScalarGridSpec(num_scal...  21 us
    pallas_call x1, Pallas kernels, widen(): pl.pallas_call(widen_kernel, grid=(steps,), in_specs=specs, out_specs=spe...  18.7 us

profile of v4, /device:TPU:0, one launch (start us, length us, event | category | flops | bytes accessed | tf_op | source)
XLA Modules:
  0.0 372.9 jit_solution(3713902987221468492)
XLA Ops:
  0.7 1.5 select_select_fusion.small_ref
  2.2 0.0 copy-start.3
  2.2 87.5 %shard_map.305 = (bf16[2,1536,640]{2,1,0:T(8,128)(2,1)}, bf16[2,1536,640]{2,1,0:T(8,128)(2,1)}, bf16[2,1536,640]{2,1,0:T(8,128)(2,1)}, bf16[256,640]{1,0:T(8,128...) custom-call(bf16[128,1280]{1,0:T(8,128)(2,1)} %tok_ref.3, ...), custom_call_target="tpu_custom_call" | custom-call | tf_op jit(solution)/shard_map/pallas_call | solution.py:909
  89.7 0.0 copy-done.3
  89.7 0.6 reshape.76.bias_ref
  90.3 21.0 %shard_map.306 = (f32[256,1280]{1,0:T(8,128)}, bf16[256,1280]{1,0:T(8,128)(2,1)}, bf16[256,1280]{1,0:T(8,128)(2,1)}, f32[256,1280]{1,0:T(8,128)}, f32[256,1280]{...) custom-call(s32[1]{0:T(128)} %bitcast.side_ref, ...), custom_call_target="tpu_custom_call" | custom-call | tf_op jit(solution)/shard_map/pallas_call | solution.py:1761
  111.3 240.0 %shard_map.307 = (bf16[2560,1280]{1,0:T(8,128)(2,1)}, bf16[640,1280]{1,0:T(8,128)(2,1)}, bf16[640,5120]{1,0:T(8,128)(2,1)}, bf16[640,1280]{1,0:T(8,128)(2,1)}, b...) custom-call(bf16[2560,1280]{1,0:T(8,128)(2,1)} %get-tuple-element.61, ...), custom_call_target="tpu_custom_call" | custom-call | tf_op jit(solution)/shard_map/pallas_call | solution.py:1611
  351.4 0.0 copy-start.2
  351.4 0.0 copy-start.1
  351.4 0.0 copy-start
  351.4 18.7 %shard_map.308 = (f32[2560,1280]{1,0:T(8,128)}, f32[640,1280]{1,0:T(8,128)}, f32[640,5120]{1,0:T(8,128)}, f32[640,1280]{1,0:T(8,128)}, f32[640,1280]{1,0:T(8,128)}, /*index=5*/f32[640,1280]{1,0:T(8,128)}) custom-call(bf16[2560,1280]{1,0:T(8,128)(2,1)} %get-tuple-element.82.refs_0_, bf16[640,1280]{1,0:T(8,128)(2,1)} %get-tuple-element.83.refs_1_, ...), custom_call_target="tpu_custom_call" | custom-call | tf_op jit(solution)/shard_map/pallas_call | solution.py:1831
  370.1 0.0 copy-done.2
  370.1 0.7 slice_reduce_fusion
  370.8 0.6 reshape.80
  371.4 0.0 copy-done.1
  371.4 0.7 copy.37
  372.1 0.0 copy-done
  372.1 0.8 copy.38
  (5 shorter events, 0.0 us)
Async XLA Ops:
  2.2 87.5 %copy-start.3 = (bf16[2560]{0:T(1024)(128)(2,1)S(1)}, bf16[2560]{0:T(1024)(128)(2,1)}, u32[]{:S(2)}) copy-start(bf16[2560]{0:T(1024)(128)(2,1)} %param.29) | copy-start | bytes 15364
  351.4 18.7 %copy-start.2 = (f32[16,640]{1,0:T(8,128)S(1)}, f32[16,640]{1,0:T(8,128)}, u32[]{:S(2)}) copy-start(f32[16,640]{1,0:T(8,128)} %get-tuple-element.94) | copy-start | bytes 122884
  351.4 20.0 %copy-start.1 = (bf16[128,1280]{1,0:T(8,128)(2,1)S(1)}, bf16[128,1280]{1,0:T(8,128)(2,1)}, u32[]{:S(2)}) copy-start(bf16[128,1280]{1,0:T(8,128)(2,1)} %get-tuple-element.128) | copy-start | bytes 983044
  351.4 20.7 %copy-start = (f32[128,1280]{1,0:T(8,128)S(1)}, f32[128,1280]{1,0:T(8,128)}, u32[]{:S(2)}) copy-start(f32[128,1280]{1,0:T(8,128)} %get-tuple-element.129) | copy-start | bytes 1966084

commit v5 on v4

--- a/solution.py
+++ b/solution.py
@@ -1696,7 +1696,6 @@
     grad_bias_ref,
     ln_ref,
     own_first,
-    turned,
 ):
     f32, bf16 = jnp.float32, jnp.bfloat16
     side = side_ref[0]
@@ -1713,7 +1712,7 @@
         cot_all_ref[chunk:, :] = cot_other_ref[...]
 
         def some_rows(i, unused):
-            rows = tile(32 * i, 32, 32)
+            rows = tile(64 * i, 64, 64)
             hidden = x_ref[rows, :].astype(f32) + mixed_ref[rows, :] + small_ref[:1, :].astype(f32)
             hidden_ref[rows, :] = hidden
             normed, _ = norm_rows(hidden)
@@ -1722,10 +1721,9 @@
             ).astype(bf16)
             return unused
 
-        lax.fori_loop(0, 2 * chunk // 32, some_rows, 0)
+        lax.fori_loop(0, 2 * chunk // 64, some_rows, 0)
         own_first[:, :half] = ln_ref[:, own_cols]
         own_first[:, half:] = ln_ref[:, other_cols]
-        turned[...] = own_first[...].T
         result_ref[...] = jnp.zeros_like(result_ref)
         back_ref[...] = jnp.zeros_like(back_ref)
 
@@ -1741,7 +1739,7 @@
     grad_pre = (matmul_nt(cot, down_ref[...]) * slope).astype(bf16)
     grad_bias_ref[...] = jnp.sum(grad_pre.astype(f32), axis=0, keepdims=True)
     grad_down_ref[...] = matmul_tn(act, cot).astype(bf16)
-    grad_up_ref[...] = matmul(turned[...], grad_pre).astype(bf16)
+    grad_up_ref[...] = matmul_tn(own_first[...], grad_pre).astype(bf16)
     back_ref[:, own_cols] += matmul_nt(grad_pre, up_own_ref[...])
     back_ref[:, other_cols] += matmul_nt(grad_pre, up_other_ref[...])
 
@@ -1788,7 +1786,6 @@
             scratch_shapes=[
                 pltpu.VMEM((rows, width), bf16),
                 pltpu.VMEM((rows, width), bf16),
-                pltpu.VMEM((width, rows), bf16),
             ],
         ),
         out_shape=[

time: 373 us -> 372 us (level)
  no operation moved by 1% of the time
where the time goes in v5:
time: 372 us
  Pallas kernels  366 us (98%)
    pallas_call x1, Pallas kernels, tail(): pl.pallas_call(tail_kernel, out_shape=[jax.ShapeDtypeStruct((ff, width),...  240 us
    pallas_call x1, Pallas kernels, front(): pl.pallas_call(front_kernel, out_shape=[window, window, window, *[jax.Sha...  87.5 us
    pallas_call x1, Pallas kernels, feed_forward(): pl.pallas_call(ff_kernel, grid_spec=pltpu.PrefetchScalarGridSpec(num_scal...  20.1 us
    pallas_call x1, Pallas kernels, widen(): pl.pallas_call(widen_kernel, grid=(steps,), in_specs=specs, out_specs=spe...  18.7 us

profile of v5, /device:TPU:0, one launch (start us, length us, event | category | flops | bytes accessed | tf_op | source)
XLA Modules:
  0.0 372.0 jit_solution(12877414052204799152)
XLA Ops:
  0.7 1.5 select_select_fusion.small_ref
  2.2 0.0 copy-start.3
  2.2 87.5 %shard_map.305 = (bf16[2,1536,640]{2,1,0:T(8,128)(2,1)}, bf16[2,1536,640]{2,1,0:T(8,128)(2,1)}, bf16[2,1536,640]{2,1,0:T(8,128)(2,1)}, bf16[256,640]{1,0:T(8,128...) custom-call(bf16[128,1280]{1,0:T(8,128)(2,1)} %tok_ref.3, ...), custom_call_target="tpu_custom_call" | custom-call | tf_op jit(solution)/shard_map/pallas_call | solution.py:909
  89.7 0.0 copy-done.3
  89.7 0.6 reshape.76.bias_ref
  90.3 20.1 %shard_map.306 = (f32[256,1280]{1,0:T(8,128)}, bf16[256,1280]{1,0:T(8,128)(2,1)}, bf16[256,1280]{1,0:T(8,128)(2,1)}, f32[256,1280]{1,0:T(8,128)}, f32[256,1280]{...) custom-call(s32[1]{0:T(128)} %bitcast.side_ref, ...), custom_call_target="tpu_custom_call" | custom-call | tf_op jit(solution)/shard_map/pallas_call | solution.py:1759
  110.4 240.0 %shard_map.307 = (bf16[2560,1280]{1,0:T(8,128)(2,1)}, bf16[640,1280]{1,0:T(8,128)(2,1)}, bf16[640,5120]{1,0:T(8,128)(2,1)}, bf16[640,1280]{1,0:T(8,128)(2,1)}, b...) custom-call(bf16[2560,1280]{1,0:T(8,128)(2,1)} %get-tuple-element.61, ...), custom_call_target="tpu_custom_call" | custom-call | tf_op jit(solution)/shard_map/pallas_call | solution.py:1611
  350.4 0.0 copy-start.2
  350.4 0.0 copy-start.1
  350.4 0.0 copy-start
  350.5 18.7 %shard_map.308 = (f32[2560,1280]{1,0:T(8,128)}, f32[640,1280]{1,0:T(8,128)}, f32[640,5120]{1,0:T(8,128)}, f32[640,1280]{1,0:T(8,128)}, f32[640,1280]{1,0:T(8,128)}, /*index=5*/f32[640,1280]{1,0:T(8,128)}) custom-call(bf16[2560,1280]{1,0:T(8,128)(2,1)} %get-tuple-element.82.refs_0_, bf16[640,1280]{1,0:T(8,128)(2,1)} %get-tuple-element.83.refs_1_, ...), custom_call_target="tpu_custom_call" | custom-call | tf_op jit(solution)/shard_map/pallas_call | solution.py:1828
  369.1 0.0 copy-done.2
  369.1 0.7 slice_reduce_fusion
  369.8 0.6 reshape.80
  370.4 0.0 copy-done.1
  370.4 0.7 copy.37
  371.1 0.0 copy-done
  371.1 0.8 copy.38
  (5 shorter events, 0.0 us)
Async XLA Ops:
  2.2 87.5 %copy-start.3 = (bf16[2560]{0:T(1024)(128)(2,1)S(1)}, bf16[2560]{0:T(1024)(128)(2,1)}, u32[]{:S(2)}) copy-start(bf16[2560]{0:T(1024)(128)(2,1)} %param.29) | copy-start | bytes 15364
  350.4 18.7 %copy-start.2 = (f32[16,640]{1,0:T(8,128)S(1)}, f32[16,640]{1,0:T(8,128)}, u32[]{:S(2)}) copy-start(f32[16,640]{1,0:T(8,128)} %get-tuple-element.94) | copy-start | bytes 122884
  350.4 20.0 %copy-start.1 = (bf16[128,1280]{1,0:T(8,128)(2,1)S(1)}, bf16[128,1280]{1,0:T(8,128)(2,1)}, u32[]{:S(2)}) copy-start(bf16[128,1280]{1,0:T(8,128)(2,1)} %get-tuple-element.128) | copy-start | bytes 983044
  350.4 20.7 %copy-start = (f32[128,1280]{1,0:T(8,128)S(1)}, f32[128,1280]{1,0:T(8,128)}, u32[]{:S(2)}) copy-start(f32[128,1280]{1,0:T(8,128)} %get-tuple-element.129) | copy-start | bytes 1966084
